TPU v7x, 512 devices: a whole 4x8x8 slice. The times are simulated.
512 devices in a mesh: queue: 64 (over z_lo, y, core), space: 8 (over x, z_hi).
Axes of the slice: x: 4, y: 8, z: 8 (z_hi: 2, z_lo: 4; z = z_hi * 4 + z_lo), core: 2. Of those that a mesh axis runs over, the one named last changes fastest.
Arguments:
- latents: float32 [64, 384, 16], P('queue', 'space'), may hold values from -6 to 6
- fresh_noise: float32 [2, 384, 16], P(None, 'space'), may hold values from -6 to 6
- levels: int32 [64], replicated, may hold values from 1 to 1000, as said below
- modulation_weight: bfloat16 [256, 6912], P(None, 'space'), may hold values from -0.375 to 0.375
- embed_weight: bfloat16 [16, 1152], replicated, may hold values from -1.5 to 1.5
- attention_weights: bfloat16 [8, 1152, 1152], P(None, 'space')
- final_weight: bfloat16 [1152, 16], replicated, may hold values from -0.1875 to 0.1875
Outputs:
- queue_after: float32 [64, 384, 16], P('queue', 'space')
- velocity: float32 [2, 64, 384, 16], P(None, 'queue', 'space')
Inputs may be any that keep to these rules, and one draw needn't show every extreme that they name: levels rise strictly along the queue, and the last one is 1000.
All inputs are finite; a program needn't handle non-finite values.
Results may differ from a plain program's by a relative error of at most 0.034.
Values may be sent and summed in bfloat16 or wider, within the bound.
A program may use at most 64 MiB of HBM per device.

v0:
```python
import math

import jax
import jax.numpy as jnp
from jax import lax
from jax.sharding import PartitionSpec as P

HEAD = 72
FREQ = 256
STEPS = 2
REACH = 4
LEVELS = 1000


def passed_along(x, axis, by):
    peers = lax.axis_size(axis)
    pairs = [(i, i + by) for i in range(peers) if 0 <= i + by < peers]
    return lax.ppermute(x, axis, pairs)


def layer_norm(values):
    average = jnp.mean(values, -1, keepdims=True)
    centred = values - average
    variance = jnp.mean(centred * centred, -1, keepdims=True)
    return centred * lax.rsqrt(variance + 1e-06)


def time_features(level_values):
    times = level_values.astype(jnp.float32) / LEVELS
    half_size = FREQ // 2
    frequency = jnp.exp(-math.log(10000.0) * jnp.arange(half_size).astype(jnp.float32) / half_size)
    angles = (times * 1000.0)[:, None] * frequency[None, :]
    return jnp.concatenate([jnp.cos(angles), jnp.sin(angles)], -1).astype(jnp.bfloat16)


def spatial_attend(query, key_rows, values):
    scores = jnp.einsum("qhd,khd->hqk", query, key_rows, preferred_element_type=jnp.float32) * (
        1.0 / math.sqrt(HEAD)
    )
    probabilities = jax.nn.softmax(scores, axis=-1).astype(jnp.bfloat16)
    return jnp.einsum(
        "hqk,khd->qhd", probabilities, values, preferred_element_type=jnp.float32
    ).astype(jnp.bfloat16)


def temporal_attend(query, key_rows, values, usable):
    scores = jnp.einsum("shd,gshd->shg", query, key_rows, preferred_element_type=jnp.float32) * (
        1.0 / math.sqrt(HEAD)
    )
    scores = jnp.where(usable[None, None, :], scores, -1e30)
    probabilities = jax.nn.softmax(scores, axis=-1).astype(jnp.bfloat16)
    return jnp.einsum(
        "shg,gshd->shd", probabilities, values, preferred_element_type=jnp.float32
    ).astype(jnp.bfloat16)


def right_product(rows, stacked):
    return lax.dot_general(
        rows, stacked, (((1,), (1,)), ((), ())), preferred_element_type=jnp.float32
    )


def local(
    latents, fresh_noise, levels, modulation_weight, embed_weight, attention_weights, final_weight
):
    queue_index = lax.axis_index("queue")
    queue_count = lax.axis_size("queue")
    space_index = lax.axis_index("space")
    own_level = lax.dynamic_index_in_dim(levels, queue_index, keepdims=False)
    below = lax.dynamic_index_in_dim(levels, jnp.maximum(queue_index - 1, 0), keepdims=False)
    next_level = jnp.where(queue_index > 0, below, 0)
    step_size = (next_level - own_level).astype(jnp.float32) / LEVELS
    modulation_share = jnp.dot(
        time_features(own_level.reshape(1)), modulation_weight, preferred_element_type=jnp.float32
    )[0]
    conditioning = lax.all_gather(modulation_share, "space", axis=0, tiled=True)
    width = embed_weight.shape[1]
    local_width = attention_weights.shape[1]
    head_count = local_width // HEAD
    spatial_weights = jnp.concatenate(
        [attention_weights[0], attention_weights[1], attention_weights[2]], 0
    )
    temporal_weights = jnp.concatenate(
        [attention_weights[4], attention_weights[5], attention_weights[6]], 0
    )
    spatial_exit = attention_weights[3]
    temporal_exit = attention_weights[7]
    current = latents[0]
    own_rows = current.shape[0]
    row_start = space_index * own_rows
    offsets = jnp.arange(2 * REACH + 1) - REACH + queue_index
    usable = (offsets >= 0) & (offsets < queue_count)
    velocities = []
    for iteration in range(STEPS):
        frame_tokens = lax.all_gather(current.astype(jnp.bfloat16), "space", axis=0, tiled=True)
        stream_in = jnp.dot(frame_tokens, embed_weight, preferred_element_type=jnp.float32)
        total = stream_in.shape[0]
        normed = (
            layer_norm(stream_in) * (1.0 + conditioning[width : 2 * width]) + conditioning[0:width]
        ).astype(jnp.bfloat16)
        spatial_proj = right_product(normed, spatial_weights).astype(jnp.bfloat16)
        spatial_proj = spatial_proj.reshape(total, 3, head_count, HEAD)
        spatial = spatial_attend(
            spatial_proj[:, 0], spatial_proj[:, 1], spatial_proj[:, 2]
        ).reshape(total, local_width)
        own_stream = lax.dynamic_slice_in_dim(stream_in, row_start, own_rows, 0)
        stream_mid = own_stream + conditioning[2 * width : 3 * width] * lax.psum_scatter(
            jnp.dot(spatial, spatial_exit, preferred_element_type=jnp.float32).astype(jnp.bfloat16),
            "space",
            scatter_dimension=0,
            tiled=True,
        ).astype(jnp.float32)
        normed_temporal = (
            layer_norm(stream_mid) * (1.0 + conditioning[4 * width : 5 * width])
            + conditioning[3 * width : 4 * width]
        ).astype(jnp.bfloat16)
        temporal_proj = right_product(
            lax.all_gather(normed_temporal, "space", axis=0, tiled=True), temporal_weights
        ).astype(jnp.bfloat16)
        temporal_query = temporal_proj[:, :local_width].reshape(total, head_count, HEAD)
        pairs = temporal_proj[:, local_width:]
        lower = []
        upper = []
        for distance in range(1, REACH + 1):
            lower.append(passed_along(pairs, "queue", distance))
            upper.append(passed_along(pairs, "queue", -distance))
        window = jnp.stack(lower[::-1] + [pairs] + upper, 0)
        key_window = window[..., :local_width].reshape(2 * REACH + 1, total, head_count, HEAD)
        value_window = window[..., local_width:].reshape(2 * REACH + 1, total, head_count, HEAD)
        temporal = temporal_attend(temporal_query, key_window, value_window, usable).reshape(
            total, local_width
        )
        stream_out = stream_mid + conditioning[5 * width : 6 * width] * lax.psum_scatter(
            jnp.dot(temporal, temporal_exit, preferred_element_type=jnp.float32).astype(
                jnp.bfloat16
            ),
            "space",
            scatter_dimension=0,
            tiled=True,
        ).astype(jnp.float32)
        velocity = jnp.dot(
            layer_norm(stream_out).astype(jnp.bfloat16),
            final_weight,
            preferred_element_type=jnp.float32,
        )
        velocities.append(velocity)
        updated = current + step_size * velocity
        arriving = passed_along(updated, "queue", -1)
        current = jnp.where(queue_index == queue_count - 1, fresh_noise[iteration], arriving)
    return (current[None], jnp.stack(velocities, 0)[:, None])


def solution(mesh):
    in_specs = (
        P("queue", "space", None),
        P(None, "space", None),
        P(),
        P(None, "space"),
        P(),
        P(None, "space", None),
        P(),
    )
    out_specs = (P("queue", "space", None), P(None, "queue", "space", None))
    return jax.shard_map(local, mesh=mesh, in_specs=in_specs, out_specs=out_specs, check_vma=False)
```

profile of v0, /device:TPU:57, one launch (start us, length us, event | category | flops | bytes accessed | tf_op | source)
XLA Modules:
  0.0 748.3 jit_solution(239213042019450517)
XLA Ops:
  8.0 40.8 %all-gather = bf16[8,48,16]{1,2,0:T(8,128)(2,1)S(1)} all-gather(bf16[1,48,16]{1,2,0:T(8,128)(2,1)S(1)} %fusion.37), channel_id=1, replica_groups=mesh['queue'=64,'space'=8] {'space'}, dimensions={0}, use_global_device_ids=true | all-gather | bytes 13824 | tf_op jit(solution)/shard_map/all_gather | solution.py:95
  48.9 1.4 fusion.57
  53.4 47.0 %all-reduce = f32[6912]{0:T(1024)S(1)} all-reduce(f32[6912]{0:T(1024)S(1)} %dynamic-update-slice), channel_id=1, replica_groups=mesh['queue'=64,'space'=8] {'space'}, use_global_device_ids=true, to_apply=%add | all-reduce | flops 6912 | bytes 55296
  100.4 1.3 fusion.58
  102.0 1.6 slice_bitcast_fusion.2
  103.7 1.6 convolution_convert_fusion.7
  105.4 1.5 fusion.59
  106.9 1.7 convolution_convert_fusion.9
  108.6 2.4 convolution_convert_fusion.3
  111.1 98.2 %reduce-scatter.5.cloned.1.call-done = bf16[48,1152]{1,0:T(8,128)(2,1)} async-done(((bf16[384,1152]{1,0:T(8,128)(2,1)}), bf16[48,1152]{1,0:T(8,128)(2,1)}) %reduce-scatter.5.cloned.1.call-update) | async-done | bytes 110608 | tf_op jit(solution)/shard_map/reduce_scatter | solution.py:107
  210.6 45.5 %all_gather.17 = bf16[384,1152]{1,0:T(8,128)(2,1)S(1)} all-gather(bf16[48,1152]{1,0:T(8,128)(2,1)S(1)} %add_convert_fusion.5), channel_id=1, replica_groups=mesh['queue'=64,'space'=8] {'space'}, dimensions={0}, use_global_device_ids=true | all-gather | bytes 995328 | tf_op jit(solution)/shard_map/all_gather | solution.py:118
  256.9 4.2 collective-permute-start
  261.1 9.6 %collective-permute-start.1 = (bf16[384,288]{0,1:T(8,128)(2,1)S(1)}, bf16[384,288]{0,1:T(8,128)(2,1)S(1)}, u32[]{:S(2)}, u32[]{:S(2)}) collective-permute-start(bf16[384,288]{0,1:T(8,128)(2,1)S(1)} %slice.136), channel_id=1, source_target_pairs={{0,24},{8,32},{16,40},{24,48},{32,56},{40,64},{48,72},{56,80},{64,... | collective-permute-start | bytes 663560 | tf_op jit(solution)/shard_map/ppermute | solution.py:18
  270.7 4.3 collective-permute-start.2
  275.0 1.9 collective-permute-start.3
  276.9 2.4 collective-permute-start.4
  279.4 1.9 collective-permute-start.5
  281.4 3.4 collective-permute-done.1
  284.7 1.9 collective-permute-start.6
  286.7 4.5 collective-permute-start.7
  291.5 6.2 collective-permute-done.6
  297.8 2.9 collective-permute-done.7
  301.6 2.4 convolution_convert_fusion.2
  305.2 91.4 %reduce-scatter.7.cloned.1.call-done = bf16[48,1152]{1,0:T(8,128)(2,1)} async-done(((bf16[384,1152]{1,0:T(8,128)(2,1)}), bf16[48,1152]{1,0:T(8,128)(2,1)}) %reduce-scatter.7.cloned.1.call-update) | async-done | bytes 110608 | tf_op jit(solution)/shard_map/reduce_scatter | solution.py:133
  399.9 4.4 collective-permute-start.8
  404.3 2.8 collective-permute-done.8
  407.8 37.3 %all-gather.1 = bf16[8,48,16]{1,2,0:T(8,128)(2,1)S(1)} all-gather(bf16[1,48,16]{1,2,0:T(8,128)(2,1)S(1)} %convert_bitcast_fusion), channel_id=1, replica_groups=mesh['queue'=64,'space'=8] {'space'}, dimensions={0}, use_global_device_ids=true | all-gather | bytes 13824 | tf_op jit(solution)/shard_map/all_gather | solution.py:95
  446.2 2.8 convolution_convert_fusion.5
  449.0 1.5 fusion.61
  450.5 1.7 convolution_convert_fusion.8
  452.2 2.4 convolution_convert_fusion.1
  454.7 87.7 %reduce-scatter.9.cloned.1.call-done = bf16[48,1152]{1,0:T(8,128)(2,1)} async-done(((bf16[384,1152]{1,0:T(8,128)(2,1)}), bf16[48,1152]{1,0:T(8,128)(2,1)}) %reduce-scatter.9.cloned.1.call-update) | async-done | bytes 110608 | tf_op jit(solution)/shard_map/reduce_scatter | solution.py:107
  543.7 45.9 %all_gather.19 = bf16[384,1152]{1,0:T(8,128)(2,1)S(1)} all-gather(bf16[48,1152]{1,0:T(8,128)(2,1)S(1)} %add_convert_fusion.4), channel_id=1, replica_groups=mesh['queue'=64,'space'=8] {'space'}, dimensions={0}, use_global_device_ids=true | all-gather | bytes 995328 | tf_op jit(solution)/shard_map/all_gather | solution.py:118
  590.4 2.9 collective-permute-start.9
  593.3 10.2 %collective-permute-start.10 = (bf16[384,288]{0,1:T(8,128)(2,1)S(1)}, bf16[384,288]{0,1:T(8,128)(2,1)S(1)}, u32[]{:S(2)}, u32[]{:S(2)}) collective-permute-start(bf16[384,288]{0,1:T(8,128)(2,1)S(1)} %slice.143), channel_id=1, source_target_pairs={{0,24},{8,32},{16,40},{24,48},{32,56},{40,64},{48,72},{56,80},{64,... | collective-permute-start | bytes 663560 | tf_op jit(solution)/shard_map/ppermute | solution.py:18
  603.6 4.5 collective-permute-start.11
  608.1 1.9 collective-permute-start.12
  610.0 2.4 collective-permute-start.13
  612.5 1.9 collective-permute-start.14
  614.4 3.0 collective-permute-done.10
  617.5 1.9 collective-permute-start.15
  619.4 4.5 collective-permute-start.16
  624.2 7.9 %collective-permute-done.15 = bf16[384,288]{0,1:T(8,128)(2,1)S(1)} collective-permute-done((bf16[384,288]{0,1:T(8,128)(2,1)S(1)}, bf16[384,288]{0,1:T(8,128)(2,1)S(1)}, u32[]{:S(2)}, u32[]{:S(2)}) %collective-permute-start.15) | collective-permute-done | bytes 221216 | tf_op jit(solution)/shard_map/ppermute | solution.py:18
  632.2 1.6 collective-permute-done.16
  634.7 2.4 convolution_convert_fusion
  637.1 93.7 %reduce-scatter.11.cloned.1.call-done = bf16[48,1152]{1,0:T(8,128)(2,1)} async-done(((bf16[384,1152]{1,0:T(8,128)(2,1)}), bf16[48,1152]{1,0:T(8,128)(2,1)}) %reduce-scatter.11.cloned.1.call-update) | async-done | bytes 110608 | tf_op jit(solution)/shard_map/reduce_scatter | solution.py:133
  734.1 4.2 collective-permute-start.17
  738.9 2.3 collective-permute-done.17
  (124 shorter events, 19.4 us)
Async XLA Ops:
  7.2 43.8 %copy-start = (bf16[256,864]{0,1:T(8,128)(2,1)S(1)}, bf16[256,864]{0,1:T(8,128)(2,1)}, u32[]{:S(2)}) copy-start(bf16[256,864]{0,1:T(8,128)(2,1)} %param.10) | copy-start | bytes 1327108
  7.2 202.1 %reduce-scatter.5.cloned.1.call-start = ((), (), s32[]{:S(2)}) async-start(), calls=%async_computation.4 | async-start | bytes 995328 | tf_op jit(solution)/shard_map/reduce_scatter | solution.py:107
  100.4 3.3 copy-start.8
  100.4 3.3 copy-start.10
  103.7 1.7 copy-start.1
  103.7 1.7 copy-start.2
  103.7 1.7 copy-start.3
  111.0 285.6 %reduce-scatter.7.cloned.1.call-start = ((), (), s32[]{:S(2)}) async-start(), calls=%async_computation.5 | async-start | bytes 995328 | tf_op jit(solution)/shard_map/reduce_scatter | solution.py:133
  256.9 22.5 %collective-permute-start = (bf16[384,288]{0,1:T(8,128)(2,1)S(1)}, bf16[384,288]{0,1:T(8,128)(2,1)S(1)}, u32[]{:S(2)}, u32[]{:S(2)}) collective-permute-start(bf16[384,288]{0,1:T(8,128)(2,1)S(1)} %slice.136), channel_id=1, source_target_pairs={{0,32},{8,40},{16,48},{24,56},{32,64},{40,72},{48,80},{56,88},{64,... | collective-permute-start | bytes 663560 | tf_op jit(solution)/shard_map/ppermute | solution.py:18
  261.1 23.6 %collective-permute-start.1 = (bf16[384,288]{0,1:T(8,128)(2,1)S(1)}, bf16[384,288]{0,1:T(8,128)(2,1)S(1)}, u32[]{:S(2)}, u32[]{:S(2)}) collective-permute-start(bf16[384,288]{0,1:T(8,128)(2,1)S(1)} %slice.136), channel_id=1, source_target_pairs={{0,24},{8,32},{16,40},{24,48},{32,56},{40,64},{48,72},{56,80},{64,... | collective-permute-start | bytes 663560 | tf_op jit(solution)/shard_map/ppermute | solution.py:18
  270.7 16.0 %collective-permute-start.2 = (bf16[384,288]{0,1:T(8,128)(2,1)S(1)}, bf16[384,288]{0,1:T(8,128)(2,1)S(1)}, u32[]{:S(2)}, u32[]{:S(2)}) collective-permute-start(bf16[384,288]{0,1:T(8,128)(2,1)S(1)} %slice.136), channel_id=1, source_target_pairs={{0,16},{8,24},{16,32},{24,40},{32,48},{40,56},{48,64},{56,72},{64,... | collective-permute-start | bytes 663560 | tf_op jit(solution)/shard_map/ppermute | solution.py:18
  275.0 16.3 %collective-permute-start.3 = (bf16[384,288]{0,1:T(8,128)(2,1)S(1)}, bf16[384,288]{0,1:T(8,128)(2,1)S(1)}, u32[]{:S(2)}, u32[]{:S(2)}) collective-permute-start(bf16[384,288]{0,1:T(8,128)(2,1)S(1)} %slice.136), channel_id=1, source_target_pairs={{0,8},{8,16},{16,24},{24,32},{32,40},{40,48},{48,56},{56,64},{64,7... | collective-permute-start | bytes 663560 | tf_op jit(solution)/shard_map/ppermute | solution.py:18
  276.9 14.4 %collective-permute-start.4 = (bf16[384,288]{0,1:T(8,128)(2,1)S(1)}, bf16[384,288]{0,1:T(8,128)(2,1)S(1)}, u32[]{:S(2)}, u32[]{:S(2)}) collective-permute-start(bf16[384,288]{0,1:T(8,128)(2,1)S(1)} %slice.136), channel_id=1, source_target_pairs={{8,0},{16,8},{24,16},{32,24},{40,32},{48,40},{56,48},{64,56},{72,6... | collective-permute-start | bytes 663560 | tf_op jit(solution)/shard_map/ppermute | solution.py:18
  279.4 12.0 %collective-permute-start.5 = (bf16[384,288]{0,1:T(8,128)(2,1)S(1)}, bf16[384,288]{0,1:T(8,128)(2,1)S(1)}, u32[]{:S(2)}, u32[]{:S(2)}) collective-permute-start(bf16[384,288]{0,1:T(8,128)(2,1)S(1)} %slice.136), channel_id=1, source_target_pairs={{16,0},{24,8},{32,16},{40,24},{48,32},{56,40},{64,48},{72,56},{80,... | collective-permute-start | bytes 663560 | tf_op jit(solution)/shard_map/ppermute | solution.py:18
  284.7 13.0 %collective-permute-start.6 = (bf16[384,288]{0,1:T(8,128)(2,1)S(1)}, bf16[384,288]{0,1:T(8,128)(2,1)S(1)}, u32[]{:S(2)}, u32[]{:S(2)}) collective-permute-start(bf16[384,288]{0,1:T(8,128)(2,1)S(1)} %slice.136), channel_id=1, source_target_pairs={{24,0},{32,8},{40,16},{48,24},{56,32},{64,40},{72,48},{80,56},{88,... | collective-permute-start | bytes 663560 | tf_op jit(solution)/shard_map/ppermute | solution.py:18
  286.7 13.9 %collective-permute-start.7 = (bf16[384,288]{0,1:T(8,128)(2,1)S(1)}, bf16[384,288]{0,1:T(8,128)(2,1)S(1)}, u32[]{:S(2)}, u32[]{:S(2)}) collective-permute-start(bf16[384,288]{0,1:T(8,128)(2,1)S(1)} %slice.136), channel_id=1, source_target_pairs={{32,0},{40,8},{48,16},{56,24},{64,32},{72,40},{80,48},{88,56},{96,... | collective-permute-start | bytes 663560 | tf_op jit(solution)/shard_map/ppermute | solution.py:18
  301.3 97.4 %copy-start.4 = (bf16[1152,16]{0,1:T(8,128)(2,1)S(1)}, bf16[1152,16]{0,1:T(8,128)(2,1)}, u32[]{:S(2)}) copy-start(bf16[1152,16]{0,1:T(8,128)(2,1)} %param.13) | copy-start | bytes 110596
  301.3 97.4 %copy-start.6 = (f32[1,48,16]{1,2,0:T(8,128)S(1)}, f32[1,48,16]{1,2,0:T(8,128)}, u32[]{:S(2)}) copy-start(f32[1,48,16]{1,2,0:T(8,128)} %param.7) | copy-start | bytes 9220
  301.5 143.7 %copy-start.5 = (bf16[16,1152]{1,0:T(8,128)(2,1)S(1)}, bf16[16,1152]{1,0:T(8,128)(2,1)}, u32[]{:S(2)}) copy-start(bf16[16,1152]{1,0:T(8,128)(2,1)} %param.11) | copy-start | bytes 110596
  304.0 238.4 %reduce-scatter.9.cloned.1.call-start = ((), (), s32[]{:S(2)}) async-start(), calls=%async_computation.6 | async-start | bytes 995328 | tf_op jit(solution)/shard_map/reduce_scatter | solution.py:107
  399.9 46.3 %copy-start.9 = (f32[1152]{0:T(1024)S(1)}, f32[1152]{0:T(1024)}, u32[]{:S(2)}) copy-start(f32[1152]{0:T(1024)} %copy-done.8) | copy-start | bytes 13828
  399.9 46.3 %copy-start.11 = (f32[1152]{0:T(1024)S(1)}, f32[1152]{0:T(1024)}, u32[]{:S(2)}) copy-start(f32[1152]{0:T(1024)} %copy-done.10) | copy-start | bytes 13828
  399.9 7.2 collective-permute-start.8
  454.6 276.2 %reduce-scatter.11.cloned.1.call-start = ((), (), s32[]{:S(2)}) async-start(), calls=%async_computation.7 | async-start | bytes 995328 | tf_op jit(solution)/shard_map/reduce_scatter | solution.py:133
  590.4 22.0 %collective-permute-start.9 = (bf16[384,288]{0,1:T(8,128)(2,1)S(1)}, bf16[384,288]{0,1:T(8,128)(2,1)S(1)}, u32[]{:S(2)}, u32[]{:S(2)}) collective-permute-start(bf16[384,288]{0,1:T(8,128)(2,1)S(1)} %slice.143), channel_id=1, source_target_pairs={{0,32},{8,40},{16,48},{24,56},{32,64},{40,72},{48,80},{56,88},{64,... | collective-permute-start | bytes 663560 | tf_op jit(solution)/shard_map/ppermute | solution.py:18
  593.3 24.1 %collective-permute-start.10 = (bf16[384,288]{0,1:T(8,128)(2,1)S(1)}, bf16[384,288]{0,1:T(8,128)(2,1)S(1)}, u32[]{:S(2)}, u32[]{:S(2)}) collective-permute-start(bf16[384,288]{0,1:T(8,128)(2,1)S(1)} %slice.143), channel_id=1, source_target_pairs={{0,24},{8,32},{16,40},{24,48},{32,56},{40,64},{48,72},{56,80},{64,... | collective-permute-start | bytes 663560 | tf_op jit(solution)/shard_map/ppermute | solution.py:18
  603.6 15.9 %collective-permute-start.11 = (bf16[384,288]{0,1:T(8,128)(2,1)S(1)}, bf16[384,288]{0,1:T(8,128)(2,1)S(1)}, u32[]{:S(2)}, u32[]{:S(2)}) collective-permute-start(bf16[384,288]{0,1:T(8,128)(2,1)S(1)} %slice.143), channel_id=1, source_target_pairs={{0,16},{8,24},{16,32},{24,40},{32,48},{40,56},{48,64},{56,72},{64,... | collective-permute-start | bytes 663560 | tf_op jit(solution)/shard_map/ppermute | solution.py:18
  608.1 16.0 %collective-permute-start.12 = (bf16[384,288]{0,1:T(8,128)(2,1)S(1)}, bf16[384,288]{0,1:T(8,128)(2,1)S(1)}, u32[]{:S(2)}, u32[]{:S(2)}) collective-permute-start(bf16[384,288]{0,1:T(8,128)(2,1)S(1)} %slice.143), channel_id=1, source_target_pairs={{0,8},{8,16},{16,24},{24,32},{32,40},{40,48},{48,56},{56,64},{64,7... | collective-permute-start | bytes 663560 | tf_op jit(solution)/shard_map/ppermute | solution.py:18
  610.0 14.1 %collective-permute-start.13 = (bf16[384,288]{0,1:T(8,128)(2,1)S(1)}, bf16[384,288]{0,1:T(8,128)(2,1)S(1)}, u32[]{:S(2)}, u32[]{:S(2)}) collective-permute-start(bf16[384,288]{0,1:T(8,128)(2,1)S(1)} %slice.143), channel_id=1, source_target_pairs={{8,0},{16,8},{24,16},{32,24},{40,32},{48,40},{56,48},{64,56},{72,6... | collective-permute-start | bytes 663560 | tf_op jit(solution)/shard_map/ppermute | solution.py:18
  612.5 11.7 %collective-permute-start.14 = (bf16[384,288]{0,1:T(8,128)(2,1)S(1)}, bf16[384,288]{0,1:T(8,128)(2,1)S(1)}, u32[]{:S(2)}, u32[]{:S(2)}) collective-permute-start(bf16[384,288]{0,1:T(8,128)(2,1)S(1)} %slice.143), channel_id=1, source_target_pairs={{16,0},{24,8},{32,16},{40,24},{48,32},{56,40},{64,48},{72,56},{80,... | collective-permute-start | bytes 663560 | tf_op jit(solution)/shard_map/ppermute | solution.py:18
  617.5 14.7 %collective-permute-start.15 = (bf16[384,288]{0,1:T(8,128)(2,1)S(1)}, bf16[384,288]{0,1:T(8,128)(2,1)S(1)}, u32[]{:S(2)}, u32[]{:S(2)}) collective-permute-start(bf16[384,288]{0,1:T(8,128)(2,1)S(1)} %slice.143), channel_id=1, source_target_pairs={{24,0},{32,8},{40,16},{48,24},{56,32},{64,40},{72,48},{80,56},{88,... | collective-permute-start | bytes 663560 | tf_op jit(solution)/shard_map/ppermute | solution.py:18
  619.4 14.4 %collective-permute-start.16 = (bf16[384,288]{0,1:T(8,128)(2,1)S(1)}, bf16[384,288]{0,1:T(8,128)(2,1)S(1)}, u32[]{:S(2)}, u32[]{:S(2)}) collective-permute-start(bf16[384,288]{0,1:T(8,128)(2,1)S(1)} %slice.143), channel_id=1, source_target_pairs={{32,0},{40,8},{48,16},{56,24},{64,32},{72,40},{80,48},{88,56},{96,... | collective-permute-start | bytes 663560 | tf_op jit(solution)/shard_map/ppermute | solution.py:18
  634.5 98.4 %copy-start.7 = (f32[2,48,16]{1,2,0:T(8,128)S(1)}, f32[2,48,16]{1,2,0:T(8,128)}, u32[]{:S(2)}) copy-start(f32[2,48,16]{1,2,0:T(8,128)} %param.8) | copy-start | bytes 18436
  734.1 7.1 collective-permute-start.17
Sparse Core Ops, SparseCore 0:
  111.2 98.0 reduce-scatter.4
  304.1 92.4 reduce-scatter.6
  454.7 87.5 reduce-scatter.8
  637.3 93.5 reduce-scatter.10
where the time goes:
time: 751 us; the launch traced here: 748 us
  waiting for transfers between devices  401 us (53%)
  blocking collectives  216 us (29%)
  starting transfers between devices  69.8 us (9%)
  matrix products  26.2 us (3%)
  between operations  17 us (2%)
  other arithmetic  11.7 us (2%)
    reduce_scatter x2, waiting for transfers between devices, local(): lax.psum_scatter(jnp.dot(spatial, spatial_exit, preferred_element_type=jn...  186 us
    reduce_scatter x2, waiting for transfers between devices, local(): lax.psum_scatter(jnp.dot(temporal, temporal_exit, preferred_element_type=...  185 us
    all_gather x2, blocking collectives, local(): lax.all_gather(normed_temporal, 'space', axis=0, tiled=True)  91.4 us
    all_gather x2, blocking collectives, local(): lax.all_gather(current.astype(jnp.bfloat16), 'space', axis=0, tiled=True)  78.1 us
    ppermute x18, starting transfers between devices, passed_along(): return lax.ppermute(x, axis, pairs)  69.6 us
    unnamed x1, blocking collectives  47 us
    ppermute x18, waiting for transfers between devices, passed_along(): return lax.ppermute(x, axis, pairs)  30.2 us
  transfers between devices with their start and end apart: 22, of which 12 were waited for; matrix products, arithmetic and copies ran while one was open for 0% of the time, Pallas kernels for 0%

commit v1 on v0

v1 whole, which is shorter than its diff:
```python
import functools
import math

import jax
import jax.numpy as jnp
from jax import lax
from jax.experimental import pallas as pl
from jax.experimental.pallas import tpu as pltpu
from jax.sharding import PartitionSpec as P

HEAD = 72
FREQ = 256
STEPS = 2
REACH = 4
LEVELS = 1000
D = 1152
ROWS = 48
NX = 4
NY = 8
SPACE = 8
ROUNDS = 4
THIRD = 384
WINDOW = 2 * REACH + 1
SCALE = 1.0 / math.sqrt(HEAD)
MESH = pl.DeviceIdType.MESH
F32 = jnp.float32
BF16 = jnp.bfloat16
PEERS = [(dx, dz) for dx in range(NX) for dz in range(2) if (dx, dz) != (0, 0)]
PARTS = [(1, 3), (6, 2), (4, 2)]
CHIPS = [-2, -1, 1, 2]


def time_features(level_values):
    times = level_values.astype(F32) / LEVELS
    half_size = FREQ // 2
    frequency = jnp.exp(-math.log(10000.0) * jnp.arange(half_size).astype(F32) / half_size)
    angles = (times * 1000.0)[:, None] * frequency[None, :]
    return jnp.concatenate([jnp.cos(angles), jnp.sin(angles)], -1).astype(BF16)


def layer_norm(values):
    average = jnp.mean(values, -1, keepdims=True)
    centred = values - average
    variance = jnp.mean(centred * centred, -1, keepdims=True)
    return centred * lax.rsqrt(variance + 1e-06)


def dot(a, b):
    return lax.dot_general(a, b, (((1,), (0,)), ((), ())), preferred_element_type=F32)


def dot_t(a, b):
    return lax.dot_general(a, b, (((1,), (1,)), ((), ())), preferred_element_type=F32)


def kernel(
    nq,
    lat, fresh, feat, step_size, mw, emb, fin, aw,
    after, velocity,
    wf, ws, tok, zf, zcur, mods, mstage, mline, mvec, n1s, qs, ks, vs, a1s, a1r,
    h1s, n2b, q2s, a2s, hm, hmt, ub, us,
    lsem, lat_s, lat_r, mod_s, mod_r, z_s, z_r, x_s, x_r, f_s, f_r, y_s, y_r, c_s, c_r,
    a_s, a_r, n_s, n_r, b_s, b_r, u_s, u_r, v_s, v_r,
):
    q = lax.axis_index("queue")
    s = lax.axis_index("space")
    x, zh = lax.div(s, 2), lax.rem(s, 2)
    chip, core = lax.div(q, 2), lax.rem(q, 2)
    line, y = lax.div(chip, NY), lax.rem(chip, NY)
    parity = lax.rem(y, 2)
    chips = nq // 2

    def peer(dx, dz):
        return lax.rem(x + dx, NX) * 2 + lax.rem(zh + dz, 2)

    def along_y(by):
        return (line * NY + lax.rem(y + by + NY, NY)) * 2 + core

    sibling = chip * 2 + 1 - core
    ahead, behind = along_y(1 - 2 * core), along_y(2 * core - 1)
    sends = []

    def remote(src, dst, ss, rs, to_q, to_s):
        return pltpu.make_async_remote_copy(
            src_ref=src, dst_ref=dst, send_sem=ss, recv_sem=rs,
            device_id=(to_q, to_s), device_id_type=MESH,
        )

    def send(src, dst, ss, rs, to_q, to_s, when=None):
        copy = remote(src, dst, ss, rs, to_q, to_s)
        if when is None:
            copy.start()
        else:
            pl.when(when)(copy.start)
        sends.append((copy, when))

    def arrived(dst, rs, when=None):
        copy = remote(dst, dst, rs, rs, q, s)
        if when is None:
            copy.wait_recv()
        else:
            pl.when(when)(copy.wait_recv)

    loads = [pltpu.make_async_copy(aw.at[pl.ds(0, 3)], ws, lsem.at[5])]
    for m in range(5):
        loads.append(
            pltpu.make_async_copy(aw.at[3 + m], wf.at[pl.ds(3 * m, 3), 0], lsem.at[m])
        )
    for load in loads[1:]:
        load.start()
    loads[0].start()

    barrier = pltpu.get_barrier_semaphore()

    def signal(to_q, to_s):
        pl.semaphore_signal(barrier, inc=1, device_id=(to_q, to_s), device_id_type=MESH)

    for dx, dz in PEERS:
        signal(q, peer(dx, dz))
    signal(behind, s)
    signal(sibling, s)
    expected = len(PEERS) + 2
    for dc in CHIPS:
        there = (chip + dc >= 0) & (chip + dc < chips)

        @pl.when(there)
        def _(dc=dc):
            signal((chip + dc) * 2 + core, s)

        expected = expected + there.astype(jnp.int32)

    @pl.when(q < nq - 1)
    def _():
        for dx in range(NX):
            for dz in range(2):
                signal(q + 1, peer(dx, dz))

    expected = expected + jnp.where(q > 0, SPACE, 0)

    tok[0, 0] = lat[...].astype(BF16)
    zcur[...] = lat[...]
    wf[15, 0] = jnp.zeros((ROWS, D), BF16)
    mstage[...] = jnp.zeros_like(mstage)
    mstage[:, 0:864] = dot(feat[...], mw[...])
    shift = lax.rem(s * 864, D)
    mline[...] = pltpu.roll(mstage[...], shift, 1)[0:1, :]
    for t in range(3):
        for ref, (row, lane) in ((hm, (0, 1)), (hmt, (1, 0))):
            shape = ref.shape[1:]
            place = lax.broadcasted_iota(jnp.int32, shape, row)
            head = lax.broadcasted_iota(jnp.int32, shape, lane)
            at = place - (head >> 1) * ROWS
            second = (at + t * ROWS >= HEAD).astype(jnp.int32)
            ref[t] = jnp.where((at >= 0) & (at < ROWS) & (second == (head & 1)), 1.0, 0.0).astype(BF16)
    for dc in CHIPS:
        @pl.when((chip + dc < 0) | (chip + dc >= chips))
        def _(dc=dc):
            for step in range(STEPS):
                for c in range(2):
                    n2b[step, (dc + 2) * 2 + c] = jnp.zeros((ROWS, D), BF16)

    pl.semaphore_wait(barrier, expected)

    for i, (dx, dz) in enumerate(PEERS):
        back = ((-dx) % NX) * 2 + dz
        send(tok.at[0, 0], tok.at[0, back], lat_s.at[i], lat_r.at[back], q, peer(dx, dz))
    for i, (dx, dz) in enumerate(PEERS):
        back = ((-dx) % NX) * 2 + dz
        send(mline, mods.at[s], mod_s.at[i], mod_r.at[back], q, peer(dx, dz))
    mods[s] = mline[...]

    def chunk(i, p, c):
        return 4 * i + 2 * p + c

    def first(i):
        j = chunk(i, parity, core)
        send(wf.at[j, 0], wf.at[j, 1], z_s.at[i], z_r.at[i], q, peer(0, 1))
        send(wf.at[j, 0], wf.at[j, 6], x_s.at[i, 0, 0], x_r.at[i, 0, 0], q, peer(1, 0))
        send(wf.at[j, 0], wf.at[j, 2], x_s.at[i, 0, 1], x_r.at[i, 0, 1], q, peer(3, 0))

    def second(i):
        j = chunk(i, parity, core)
        arrived(wf.at[j, 1], z_r.at[i])
        send(wf.at[j, 1], wf.at[j, 7], x_s.at[i, 1, 0], x_r.at[i, 1, 0], q, peer(1, 0))
        send(wf.at[j, 1], wf.at[j, 3], x_s.at[i, 1, 1], x_r.at[i, 1, 1], q, peer(3, 0))

    def third(i):
        j = chunk(i, parity, core)
        start = 6 - 4 * core
        arrived(wf.at[j, start], x_r.at[i, 0, core])
        arrived(wf.at[j, start + 1], x_r.at[i, 1, core])
        to = lax.rem(x + 1 + 2 * core, NX) * 2 + zh
        send(wf.at[j, pl.ds(start, 2)], wf.at[j, pl.ds(4, 2)], f_s.at[i], f_r.at[i], q, to)

    def share(i, part):
        j = chunk(i, parity, core)
        at = pl.ds(*PARTS[part])
        send(wf.at[j, at], wf.at[j, at], y_s.at[i, part], y_r.at[i, part], ahead, s)
        send(wf.at[j, at], wf.at[j, at], c_s.at[i, part], c_r.at[i, part], sibling, s)

    def fourth(i):
        j = chunk(i, parity, core)
        start = 2 + 4 * core
        arrived(wf.at[j, start], x_r.at[i, 0, 1 - core])
        arrived(wf.at[j, start + 1], x_r.at[i, 1, 1 - core])
        share(i, 0)
        share(i, 1)

    def fifth(i):
        j = chunk(i, parity, core)
        arrived(wf.at[j, pl.ds(4, 2)], f_r.at[i])
        share(i, 2)

    def sixth(i):
        j = chunk(i, 1 - parity, core)
        for part in range(3):
            at = pl.ds(*PARTS[part])
            arrived(wf.at[j, at], y_r.at[i, part])
            send(wf.at[j, at], wf.at[j, at], c_s.at[i, 3 + part], c_r.at[i, 3 + part], sibling, s)

    def seventh(i):
        for half, p in ((0, parity), (3, 1 - parity)):
            j = chunk(i, p, 1 - core)
            for part in range(3):
                arrived(wf.at[j, pl.ds(*PARTS[part])], c_r.at[i, half + part])

    for load in loads[1:]:
        load.wait()
    first(0)
    first(1)

    for dx, dz in PEERS:
        arrived(mods.at[peer(dx, dz)], mod_r.at[dx * 2 + dz])
    for base in (0, 4):
        piece = base // 4 * 3
        left = [mods[base + g][:, 0:D] for g in range(4)]
        right = [mods[base + g][:, D : 2 * D] for g in range(4)]
        mvec[piece] = left[0] + left[1]
        mvec[piece + 1] = right[1] + left[2]
        mvec[piece + 2] = right[2] + left[3]

    loads[0].wait()
    for dx, dz in PEERS:
        arrived(tok.at[0, dx * 2 + dz], lat_r.at[dx * 2 + dz])

    lane = lax.broadcasted_iota(jnp.int32, (1, 144), 1)
    in_first = lane < HEAD

    def spatial(step):
        @pl.loop(0, SPACE)
        def _(r):
            h0 = dot(tok[step, r], emb[...])
            n1 = layer_norm(h0) * (1.0 + mvec[1]) + mvec[0]
            n1s[r] = n1.astype(BF16)

        for index, ref in enumerate((qs, ks, vs)):
            ref[...] = dot_t(
                n1s[...].reshape(SPACE * ROWS, D), ws[index].reshape(144, D)
            ).astype(BF16)

    def attend(step):
        @pl.loop(0, 4)
        def _(b):
            rows = pl.ds(pl.multiple_of(b * 96, 96), 96)
            query = qs[rows, :]
            heads = []
            for h in range(2):
                mine = in_first if h == 0 else ~in_first
                scores = dot_t(jnp.where(mine, query, jnp.zeros_like(query)), ks[...]) * SCALE
                e = jnp.exp(scores - jnp.max(scores, -1, keepdims=True))
                p = (e / jnp.sum(e, -1, keepdims=True)).astype(BF16)
                heads.append(dot(p, vs[...]))
            a1 = jnp.where(in_first, heads[0], heads[1]).astype(BF16)
            a1s[step, pl.ds(b * 2, 2)] = a1.reshape(2, ROWS, 144)

        for i, (dx, dz) in enumerate(PEERS):
            back = ((-dx) % NX) * 2 + dz
            send(a1s.at[step, dx * 2 + dz], a1r.at[step, back],
                 a_s.at[step, i], a_r.at[step, back], q, peer(dx, dz))
        a1r[step, 0] = a1s[step, 0]

    def leave(step):
        for dx, dz in PEERS:
            arrived(a1r.at[step, dx * 2 + dz], a_r.at[step, dx * 2 + dz])

    def middle(step):
        o1 = dot(a1r[step, 0], wf[0:3, 0].reshape(144, D))
        for r in range(1, SPACE):
            o1 = o1 + dot(a1r[step, r], wf[0:3, r].reshape(144, D))
        h1 = dot(tok[step, 0], emb[...]) + mvec[2] * o1
        h1s[...] = h1
        n2 = layer_norm(h1) * (1.0 + mvec[4]) + mvec[3]
        n2b[step, 4 + core] = n2.astype(BF16)
        for i, dc in enumerate(CHIPS):
            there = (chip + dc >= 0) & (chip + dc < chips)
            own = n2b.at[step, 4 + core]
            send(own, n2b.at[step, (2 - dc) * 2 + core], n_s.at[step, i], n_r.at[step, 3 - i],
                 (chip + dc) * 2 + core, s, there)
        send(n2b.at[step, 4 + core], n2b.at[step, 4 + core], b_s.at[step, 4], b_r.at[step, 4], sibling, s)

    def around(step):
        order = [1, 2, 0, 3]
        for i in order:
            dc = CHIPS[i]
            there = (chip + dc >= 0) & (chip + dc < chips)
            slot = (dc + 2) * 2 + core
            arrived(n2b.at[step, slot], n_r.at[step, i], there)
            wanted = there
            if dc == -2:
                wanted = there & (core == 1)
            if dc == 2:
                wanted = there & (core == 0)
            send(n2b.at[step, slot], n2b.at[step, slot], b_s.at[step, i], b_r.at[step, i],
                 sibling, s, wanted)
        arrived(n2b.at[step, 5 - core], b_r.at[step, 4])
        for i in order:
            dc = CHIPS[i]
            there = (chip + dc >= 0) & (chip + dc < chips)
            slot = (dc + 2) * 2 + 1 - core
            wanted = there
            if dc == -2:
                wanted = there & (core == 0)
            if dc == 2:
                wanted = there & (core == 1)
            arrived(n2b.at[step, slot], b_r.at[step, i], wanted)

    def queries(step):
        @pl.loop(0, 3)
        def _(t):
            q2s[t] = dot_t(n2b[step, 4 + core], wf[3 + t].reshape(THIRD, D)).astype(BF16)

    def temporal(step):
        window = n2b[step, pl.ds(core, WINDOW)].reshape(WINDOW * ROWS, D)

        def keys(t, total):
            k2 = dot_t(window, wf[6 + t].reshape(THIRD, D)).astype(BF16)
            product = k2.reshape(WINDOW, ROWS, THIRD).astype(F32) * q2s[t].astype(F32)[None]
            return total + dot(product.astype(BF16).reshape(WINDOW * ROWS, THIRD), hm[t])

        scores = lax.fori_loop(0, 3, keys, jnp.zeros((WINDOW * ROWS, 128), F32)) * SCALE
        scores = scores.reshape(WINDOW, ROWS, 128)
        block = lax.broadcasted_iota(jnp.int32, scores.shape, 0) - REACH + q
        scores = jnp.where((block >= 0) & (block < nq), scores, -1e30)
        e = jnp.exp(scores - jnp.max(scores, 0, keepdims=True))
        p = (e / jnp.sum(e, 0, keepdims=True)).astype(BF16).reshape(WINDOW * ROWS, 128)

        @pl.loop(0, 3)
        def _(t):
            v2 = dot_t(window, wf[9 + t].reshape(THIRD, D)).astype(BF16).astype(F32)
            spread = dot(p, hmt[t])
            a2s[t] = jnp.sum((spread * v2).reshape(WINDOW, ROWS, THIRD), 0).astype(BF16)

    def final(step):
        o2 = dot(a2s[0], wf[12].reshape(THIRD, D))
        for t in range(1, 3):
            o2 = o2 + dot(a2s[t], wf[12 + t].reshape(THIRD, D))
        h2 = h1s[...] + mvec[5] * o2
        v = dot(layer_norm(h2).astype(BF16), fin[...])
        velocity[step] = v
        u = zcur[...] + step_size[0:1, 0:1] * v
        us[step] = u
        head = q > 0
        tail = q == nq - 1
        if step < STEPS - 1:
            ub[0] = u.astype(BF16)
            ub[1] = fresh[step].astype(BF16)
            for dx in range(NX):
                for dz in range(2):
                    back = ((-dx) % NX) * 2 + dz
                    here = dx * 2 + dz
                    send(ub.at[0], tok.at[step + 1, back], u_s.at[0, here], u_r.at[back],
                         q - 1, peer(dx, dz), head)
                    if here:
                        send(ub.at[1], tok.at[step + 1, back], u_s.at[1, here], u_r.at[back],
                             q, peer(dx, dz), tail)
        send(us.at[step], zf.at[step], v_s.at[step], v_r.at[step], q - 1, s, head)

    def arrive(step):
        tail = q == nq - 1
        if step < STEPS - 1:
            for here in range(1, SPACE):
                arrived(tok.at[step + 1, here], u_r.at[here])
            arrived(tok.at[step + 1, 0], u_r.at[0], ~tail)

            @pl.when(tail)
            def _():
                tok[step + 1, 0] = fresh[step].astype(BF16)

        arrived(zf.at[step], v_r.at[step], ~tail)

        @pl.when(tail)
        def _():
            zf[step] = fresh[step]

    spatial(0)
    second(0)
    third(0)
    first(2)
    attend(0)
    fourth(0)
    second(1)
    fifth(0)
    third(1)
    first(3)
    leave(0)
    sixth(0)
    fourth(1)
    second(2)
    fifth(1)
    third(2)
    seventh(0)
    middle(0)
    sixth(1)
    fourth(2)
    second(3)
    fifth(2)
    third(3)
    seventh(1)
    queries(0)
    around(0)
    fourth(3)
    sixth(2)
    fifth(3)
    seventh(2)
    temporal(0)
    sixth(3)
    seventh(3)
    final(0)
    arrive(0)
    zcur[...] = zf[0]
    spatial(1)
    attend(1)
    leave(1)
    middle(1)
    queries(1)
    around(1)
    temporal(1)
    final(1)
    arrive(1)
    after[...] = zf[1]

    for copy, when in sends:
        if when is None:
            copy.wait_send()
        else:
            pl.when(when)(copy.wait_send)


def solution(mesh):
    nq = mesh.shape["queue"]

    def local(latents, fresh_noise, levels, modulation_weight, embed_weight, attention_weights, final_weight):
        q = lax.axis_index("queue")
        own = lax.dynamic_index_in_dim(levels, q, keepdims=False)
        below = lax.dynamic_index_in_dim(levels, jnp.maximum(q - 1, 0), keepdims=False)
        below = jnp.where(q > 0, below, 0)
        step_size = jnp.broadcast_to((below - own).astype(F32) / LEVELS, (8, 128))
        feat = jnp.broadcast_to(time_features(own.reshape(1)), (8, FREQ))
        dma = pltpu.SemaphoreType.DMA
        vmem = pl.BlockSpec(memory_space=pltpu.VMEM)
        after, velocity = pl.pallas_call(
            functools.partial(kernel, nq),
            out_shape=(
                jax.ShapeDtypeStruct((ROWS, 16), F32),
                jax.ShapeDtypeStruct((STEPS, ROWS, 16), F32),
            ),
            in_specs=[vmem] * 7 + [pl.BlockSpec(memory_space=pl.ANY)],
            out_specs=(vmem, vmem),
            scratch_shapes=[
                pltpu.VMEM((16, SPACE, ROWS, D), BF16),
                pltpu.VMEM((3, 3, ROWS, D), BF16),
                pltpu.VMEM((STEPS, SPACE, ROWS, 16), BF16),
                pltpu.VMEM((STEPS, ROWS, 16), F32),
                pltpu.VMEM((ROWS, 16), F32),
                pltpu.VMEM((SPACE, 1, 2 * D), F32),
                pltpu.VMEM((8, 2 * D), F32),
                pltpu.VMEM((1, 2 * D), F32),
                pltpu.VMEM((6, 1, D), F32),
                pltpu.VMEM((SPACE, ROWS, D), BF16),
                pltpu.VMEM((SPACE * ROWS, 144), BF16),
                pltpu.VMEM((SPACE * ROWS, 144), BF16),
                pltpu.VMEM((SPACE * ROWS, 144), BF16),
                pltpu.VMEM((STEPS, SPACE, ROWS, 144), BF16),
                pltpu.VMEM((STEPS, SPACE, ROWS, 144), BF16),
                pltpu.VMEM((ROWS, D), F32),
                pltpu.VMEM((STEPS, 10, ROWS, D), BF16),
                pltpu.VMEM((3, ROWS, THIRD), BF16),
                pltpu.VMEM((3, ROWS, THIRD), BF16),
                pltpu.VMEM((3, THIRD, 128), BF16),
                pltpu.VMEM((3, 128, THIRD), BF16),
                pltpu.VMEM((2, ROWS, 16), BF16),
                pltpu.VMEM((STEPS, ROWS, 16), F32),
                dma((6,)),
                dma((7,)), dma((SPACE,)),
                dma((7,)), dma((SPACE,)),
                dma((ROUNDS,)), dma((ROUNDS,)),
                dma((ROUNDS, 2, 2)), dma((ROUNDS, 2, 2)),
                dma((ROUNDS,)), dma((ROUNDS,)),
                dma((ROUNDS, 3)), dma((ROUNDS, 3)),
                dma((ROUNDS, 6)), dma((ROUNDS, 6)),
                dma((STEPS, 7)), dma((STEPS, SPACE)),
                dma((STEPS, 4)), dma((STEPS, 4)),
                dma((STEPS, 5)), dma((STEPS, 5)),
                dma((2, SPACE)), dma((SPACE,)),
                dma((STEPS,)), dma((STEPS,)),
            ],
            compiler_params=pltpu.CompilerParams(
                collective_id=0, has_side_effects=True, vmem_limit_bytes=56 << 20
            ),
            name="denoise",
        )(
            latents[0], fresh_noise, feat, step_size, modulation_weight, embed_weight,
            final_weight, attention_weights.reshape(8, 3, ROWS, D),
        )
        return after[None], velocity[:, None]

    in_specs = (
        P("queue", "space", None),
        P(None, "space", None),
        P(),
        P(None, "space"),
        P(),
        P(None, "space", None),
        P(),
    )
    out_specs = (P("queue", "space", None), P(None, "queue", "space", None))
    return jax.shard_map(local, mesh=mesh, in_specs=in_specs, out_specs=out_specs, check_vma=False)
```

time: 751 us -> 143 us (0.19)
  the two profiles are of different devices: /device:TPU:57 before, /device:TPU:201 now
where the time goes in v1:
time: 143 us; the launch traced here: 142 us
  Pallas kernels  128 us (90%)
  local copies, waits for them, and re-layouts  11.8 us (8%)
  between operations  2.61 us (2%)
    pallas_call x1, Pallas kernels, local(): pl.pallas_call(functools.partial(kernel, nq), out_shape=(jax.ShapeDtypeSt...  128 us
    unnamed x6, local copies, waits for them, and re-layouts  9.31 us

profile of v1, /device:TPU:201, one launch (start us, length us, event | category | flops | bytes accessed | tf_op | source)
XLA Modules:
  0.0 142.3 jit_solution(9118957583237781232)
XLA Ops:
  0.6 1.3 fusion
  4.0 0.6 broadcast_in_dim.16.feat
  4.6 0.6 broadcast_in_dim.17.step_size
  5.2 1.4 copy.9
  6.6 1.4 copy.10.fresh
  8.0 1.6 %copy.12.fin = bf16[1152,16]{1,0:T(8,128)(2,1)} copy(bf16[1152,16]{0,1:T(8,128)(2,1)} %param.13) | data formatting | bytes 73728 | tf_op args[6]
  9.6 2.0 %copy.11.mw = bf16[256,864]{1,0:T(8,128)(2,1)} copy(bf16[256,864]{0,1:T(8,128)(2,1)} %param.10) | data formatting | bytes 884736 | tf_op args[3]
  11.6 127.8 %denoise.1 = (f32[48,16]{1,0:T(8,128)}, f32[2,48,16]{2,1,0:T(8,128)}) custom-call(f32[48,16]{1,0:T(8,128)} %bitcast.8, f32[2,48,16]{2,1,0:T(8,128)} %copy.10.fresh, bf16[8,256]{1,0:T(8,128)(2,1)} %broadcast_in_dim.16.feat, f32[8,128]{1,0:T(8,128)} %broadcast_in_dim.17.step_size, bf16[256,864]{1,0:T(8,128)(2,1)} %copy.11.mw, bf16[16,1152]{1,0:T(8,128)(2,1)} %emb.1, ...), custom_call_target="tpu_custom_call" | custom-call | tf_op jit(solution)/shard_map/denoise/pallas_call | solution.py:461
  139.4 1.4 copy.13
  140.8 1.5 %copy.14 = f32[2,1,48,16]{2,3,1,0:T(8,128)} copy(f32[2,1,48,16]{3,2,0,1:T(8,128)} %bitcast.9) | data formatting | bytes 12288
  (2 shorter events, 0.1 us)

commit v2 on v1

v2 whole, which is shorter than its diff:
```python
import functools
import math

import jax
import jax.numpy as jnp
from jax import lax
from jax.experimental import pallas as pl
from jax.experimental.pallas import tpu as pltpu
from jax.sharding import PartitionSpec as P

HEAD = 72
FREQ = 256
STEPS = 2
REACH = 4
LEVELS = 1000
D = 1152
ROWS = 48
NX = 4
NY = 8
SPACE = 8
ROUNDS = 4
THIRD = 384
SLOTS = 2 * REACH + 2
SCALE = 1.0 / math.sqrt(HEAD)
MESH = pl.DeviceIdType.MESH
F32 = jnp.float32
BF16 = jnp.bfloat16
SLOT = {(dx, dz): dz * NX + at for dz in range(2) for at, dx in enumerate((0, 3, 1, 2))}
PEERS = [place for place in SLOT if place != (0, 0)]
PARTS = [(1, 2), (3, 1), (4, 1), (5, 2), (7, 1)]
OVER_Z = (2, 4)
CHIPS = [-2, -1, 1, 2]


def time_features(level):
    half_size = FREQ // 2
    places = lax.broadcasted_iota(jnp.int32, (8, half_size), 1).astype(F32)
    frequency = jnp.exp(-math.log(10000.0) * places / half_size)
    angles = (level.astype(F32) / LEVELS * 1000.0) * frequency
    return jnp.concatenate([jnp.cos(angles), jnp.sin(angles)], -1).astype(BF16)


def layer_norm(values):
    average = jnp.mean(values, -1, keepdims=True)
    centred = values - average
    variance = jnp.mean(centred * centred, -1, keepdims=True)
    return centred * lax.rsqrt(variance + 1e-06)


def dot(a, b):
    return lax.dot_general(a, b, (((1,), (0,)), ((), ())), preferred_element_type=F32)


def t_dot(a, b):
    return lax.dot_general(a, b, (((0,), (0,)), ((), ())), preferred_element_type=F32)


def dot_t(a, b):
    return lax.dot_general(a, b, (((1,), (1,)), ((), ())), preferred_element_type=F32)


def kernel(
    nq,
    levels, lat, fresh, mw, emb, fin, aw,
    after, velocity,
    wf, ws, tok, zf, zcur, mods, mstage, mline, mvec, n1s, qs, ks, vs, a1s, a1r,
    h1s, n2b, q2s, a2s, sc, v2s, hm, hmt, ub, us,
    lsem, lat_s, lat_r, mod_s, mod_r, z_s, z_r, x_s, x_r, f_s, f_r, y_s, y_r, c_s, c_r,
    a_s, a_r, n_s, n_r, b_s, b_r, u_s, u_r, v_s, v_r,
):
    q = lax.axis_index("queue")
    s = lax.axis_index("space")
    x, zh = lax.div(s, 2), lax.rem(s, 2)
    chip, core = lax.div(q, 2), lax.rem(q, 2)
    line, y = lax.div(chip, NY), lax.rem(chip, NY)
    parity = lax.rem(y + line, 2)
    chips = nq // 2

    def peer(dx, dz):
        return lax.rem(x + dx, NX) * 2 + lax.rem(zh + dz, 2)

    def along_y(by):
        return (line * NY + lax.rem(y + by + NY, NY)) * 2 + core

    sibling = chip * 2 + 1 - core
    lines = nq // (2 * NY)
    mirror = ((lines - 1 - line) * NY + y) * 2 + core
    beside = ((line + 1 - 2 * lax.rem(line, 2)) * NY + y) * 2 + core
    ahead, behind = along_y(1 - 2 * core), along_y(2 * core - 1)
    sends = []

    def remote(src, dst, ss, rs, to_q, to_s):
        return pltpu.make_async_remote_copy(
            src_ref=src, dst_ref=dst, send_sem=ss, recv_sem=rs,
            device_id=(to_q, to_s), device_id_type=MESH,
        )

    def send(src, dst, ss, rs, to_q, to_s, when=None):
        copy = remote(src, dst, ss, rs, to_q, to_s)
        if when is None:
            copy.start()
        else:
            pl.when(when)(copy.start)
        sends.append((copy, when))

    def arrived(dst, rs, when=None):
        copy = remote(dst, dst, rs, rs, q, s)
        if when is None:
            copy.wait_recv()
        else:
            pl.when(when)(copy.wait_recv)

    loads = [pltpu.make_async_copy(aw.at[pl.ds(0, 3)], ws, lsem.at[5])]
    for m in range(5):
        loads.append(
            pltpu.make_async_copy(aw.at[3 + m], wf.at[pl.ds(3 * m, 3), 0], lsem.at[m])
        )
    for load in loads[1:]:
        load.start()
    loads[0].start()

    barrier = pltpu.get_barrier_semaphore()

    def signal(to_q, to_s):
        pl.semaphore_signal(barrier, inc=1, device_id=(to_q, to_s), device_id_type=MESH)

    for dx, dz in PEERS:
        signal(q, peer(dx, dz))
    signal(behind, s)
    signal(beside, s)
    signal(sibling, s)
    signal(mirror, peer(0, 1))
    expected = len(PEERS) + 4
    for dc in CHIPS:
        there = (chip + dc >= 0) & (chip + dc < chips)

        @pl.when(there)
        def _(dc=dc):
            signal((chip + dc) * 2 + core, s)

        expected = expected + there.astype(jnp.int32)

    @pl.when(q < nq - 1)
    def _():
        for dx in range(NX):
            for dz in range(2):
                signal(q + 1, peer(dx, dz))

    expected = expected + jnp.where(q > 0, SPACE, 0)

    tok[0, 0] = lat[...].astype(BF16)
    zcur[...] = lat[...]
    wf[15, 0] = jnp.zeros((ROWS, D), BF16)
    mstage[...] = jnp.zeros_like(mstage)
    mstage[:, 0:864] = dot_t(time_features(levels[q]), mw[...])
    shift = lax.rem(s * 864, D)
    mline[...] = pltpu.roll(mstage[...], shift, 1)[0:1, :]
    for t in range(3):
        for ref, (row, lane) in ((hm, (0, 1)), (hmt, (1, 0))):
            shape = ref.shape[1:]
            place = lax.broadcasted_iota(jnp.int32, shape, row)
            head = lax.broadcasted_iota(jnp.int32, shape, lane)
            at = place - (head >> 1) * ROWS
            second = (at + t * ROWS >= HEAD).astype(jnp.int32)
            ref[t] = jnp.where((at >= 0) & (at < ROWS) & (second == (head & 1)), 1.0, 0.0).astype(BF16)
    for step in range(STEPS):
        n2b[step, 9 - 9 * core] = jnp.zeros((ROWS, D), BF16)
    for dc in CHIPS:
        @pl.when((chip + dc < 0) | (chip + dc >= chips))
        def _(dc=dc):
            for step in range(STEPS):
                for c in range(2):
                    n2b[step, (dc + 2) * 2 + c] = jnp.zeros((ROWS, D), BF16)

    pl.semaphore_wait(barrier, expected)

    for i, (dx, dz) in enumerate(PEERS):
        back = SLOT[-dx % NX, dz]
        send(tok.at[0, 0], tok.at[0, back], lat_s.at[i], lat_r.at[back], q, peer(dx, dz))
    for i, (dx, dz) in enumerate(PEERS):
        back = SLOT[-dx % NX, dz]
        send(mline, mods.at[s], mod_s.at[i], mod_r.at[back], q, peer(dx, dz))
    mods[s] = mline[...]

    def chunk(i, p, c):
        return 4 * i + 2 * p + c

    def own_out(i):
        j = chunk(i, parity, core)
        send(wf.at[j, 0], wf.at[j, 1], x_s.at[i, 0, 0], x_r.at[i, 0, 0], q, peer(1, 0))
        send(wf.at[j, 0], wf.at[j, 2], x_s.at[i, 0, 1], x_r.at[i, 0, 1], q, peer(3, 0))

    def cross_out(i):
        j = chunk(i, 1 - parity, core)
        send(wf.at[j, 0], wf.at[j, 4], z_s.at[i], z_r.at[i], mirror, peer(0, 1))

    def share(i, part):
        j = chunk(i, parity, core)
        at = pl.ds(*PARTS[part])
        to = beside if part in OVER_Z else ahead
        send(wf.at[j, at], wf.at[j, at], y_s.at[i, part], y_r.at[i, part], to, s)
        send(wf.at[j, at], wf.at[j, at], c_s.at[i, part], c_r.at[i, part], sibling, s)

    def onward(i, half):
        j = chunk(i, parity, core)
        base = 4 * half
        arrived(wf.at[j, base + 1], x_r.at[i, half, 0])
        arrived(wf.at[j, base + 2], x_r.at[i, half, 1])
        to = lax.rem(x + 1 + 2 * core, NX) * 2 + zh
        send(wf.at[j, base + 1 + core], wf.at[j, base + 3], f_s.at[i, half], f_r.at[i, half], q, to)
        share(i, 3 * half)

    def far_in(i, half):
        j = chunk(i, parity, core)
        arrived(wf.at[j, 4 * half + 3], f_r.at[i, half])
        share(i, 3 * half + 1)

    def cross_in(i):
        j = chunk(i, parity, core)
        arrived(wf.at[j, 4], z_r.at[i])
        send(wf.at[j, 4], wf.at[j, 5], x_s.at[i, 1, 0], x_r.at[i, 1, 0], q, peer(1, 0))
        send(wf.at[j, 4], wf.at[j, 6], x_s.at[i, 1, 1], x_r.at[i, 1, 1], q, peer(3, 0))
        share(i, 2)

    def pass_on(i, *parts):
        j = chunk(i, 1 - parity, core)
        for part in parts:
            at = pl.ds(*PARTS[part])
            arrived(wf.at[j, at], y_r.at[i, part])
            send(wf.at[j, at], wf.at[j, at], c_s.at[i, 5 + part], c_r.at[i, 5 + part], sibling, s)

    def complete(i):
        for half, p in ((0, parity), (5, 1 - parity)):
            j = chunk(i, p, 1 - core)
            for part in range(5):
                arrived(wf.at[j, pl.ds(*PARTS[part])], c_r.at[i, half + part])

    for load in loads[1:]:
        load.wait()
    own_out(0)
    cross_out(0)
    own_out(1)
    own_out(2)
    own_out(3)

    for dx, dz in PEERS:
        arrived(mods.at[peer(dx, dz)], mod_r.at[SLOT[dx, dz]])
    for base in (0, 4):
        piece = base // 4 * 3
        left = [mods[base + g][:, 0:D] for g in range(4)]
        right = [mods[base + g][:, D : 2 * D] for g in range(4)]
        mvec[piece] = left[0] + left[1]
        mvec[piece + 1] = right[1] + left[2]
        mvec[piece + 2] = right[2] + left[3]

    loads[0].wait()
    lane = lax.broadcasted_iota(jnp.int32, (1, 144), 1)
    in_first = lane < HEAD

    def embed(step, *slots):
        for r in slots:
            if step == 0 and r:
                arrived(tok.at[0, r], lat_r.at[r])
            elif r:
                arrived(tok.at[step, r], u_r.at[r])
            elif step:
                arrived(tok.at[step, 0], u_r.at[0], q < nq - 1)

                @pl.when(q == nq - 1)
                def _():
                    tok[step, 0] = fresh[step - 1].astype(BF16)

            h0 = t_dot(tok[step, r], emb[...])
            n1s[r] = (layer_norm(h0) * (1.0 + mvec[1]) + mvec[0]).astype(BF16)

    def project(*indices):
        for index in indices:
            (qs, ks, vs)[index][...] = dot_t(
                n1s[...].reshape(SPACE * ROWS, D), ws[index].reshape(144, D)
            ).astype(BF16)

    def attend(step, b):
        query = qs[b * 96 : b * 96 + 96, :]
        heads = []
        for h in range(2):
            mine = in_first if h == 0 else ~in_first
            scores = dot_t(jnp.where(mine, query, jnp.zeros_like(query)), ks[...]) * SCALE
            e = jnp.exp(scores - jnp.max(scores, -1, keepdims=True))
            p = (e * (1.0 / jnp.sum(e, -1, keepdims=True))).astype(BF16)
            heads.append(dot(p, vs[...]))
        a1 = jnp.where(in_first, heads[0], heads[1]).astype(BF16)
        a1s[step, 2 * b : 2 * b + 2] = a1.reshape(2, ROWS, 144)
        for i, (dx, dz) in enumerate(PEERS):
            if SLOT[dx, dz] // 2 == b:
                back = SLOT[-dx % NX, dz]
                send(a1s.at[step, SLOT[dx, dz]], a1r.at[step, back],
                     a_s.at[step, i], a_r.at[step, back], q, peer(dx, dz))
        if b == 0:
            a1r[step, 0] = a1s[step, 0]

    def middle(step):
        h0 = t_dot(tok[step, 0], emb[...])
        o1 = dot(a1r[step, 0], wf[0:3, 0].reshape(144, D))
        for r in range(1, SPACE):
            arrived(a1r.at[step, r], a_r.at[step, r])
            o1 = o1 + dot(a1r[step, r], wf[0:3, r].reshape(144, D))
        h1 = h0 + mvec[2] * o1
        h1s[...] = h1
        n2 = layer_norm(h1) * (1.0 + mvec[4]) + mvec[3]
        n2b[step, 4 + core] = n2.astype(BF16)
        own = n2b.at[step, 4 + core]
        send(own, own, b_s.at[step, 4], b_r.at[step, 4], sibling, s)
        for i in (1, 2, 0, 3):
            dc = CHIPS[i]
            there = (chip + dc >= 0) & (chip + dc < chips)
            send(own, n2b.at[step, (2 - dc) * 2 + core], n_s.at[step, i], n_r.at[step, 3 - i],
                 (chip + dc) * 2 + core, s, there)

    def relay(step, *chips_from):
        for i in chips_from:
            dc = CHIPS[i]
            there = (chip + dc >= 0) & (chip + dc < chips)
            slot = (dc + 2) * 2 + core
            arrived(n2b.at[step, slot], n_r.at[step, i], there)
            wanted = there
            if dc == -2:
                wanted = there & (core == 1)
            if dc == 2:
                wanted = there & (core == 0)
            send(n2b.at[step, slot], n2b.at[step, slot], b_s.at[step, i], b_r.at[step, i],
                 sibling, s, wanted)

    def relayed(step, *chips_from):
        for i in chips_from:
            dc = CHIPS[i]
            there = (chip + dc >= 0) & (chip + dc < chips)
            slot = (dc + 2) * 2 + 1 - core
            wanted = there
            if dc == -2:
                wanted = there & (core == 0)
            if dc == 2:
                wanted = there & (core == 1)
            arrived(n2b.at[step, slot], b_r.at[step, i], wanted)

    def queries(step):
        for t in range(3):
            q2s[t] = dot_t(n2b[step, 4 + core], wf[3 + t].reshape(THIRD, D)).astype(BF16)
        arrived(n2b.at[step, 5 - core], b_r.at[step, 4])

    def keys(step, *groups):
        for low, high in groups:
            count = high - low
            rows = n2b[step, low:high].reshape(count * ROWS, D)
            total = jnp.zeros((count * ROWS, 128), F32)
            for t in range(3):
                k2 = dot_t(rows, wf[6 + t].reshape(THIRD, D)).astype(BF16)
                product = k2.reshape(count, ROWS, THIRD).astype(F32) * q2s[t].astype(F32)[None]
                total = total + dot(product.astype(BF16).reshape(count * ROWS, THIRD), hm[t])
            sc[low:high] = total.reshape(count, ROWS, 128)

    def values(step, *groups):
        for low, high in groups:
            count = high - low
            rows = n2b[step, low:high].reshape(count * ROWS, D)
            for t in range(3):
                v2 = dot_t(rows, wf[9 + t].reshape(THIRD, D)).astype(BF16)
                v2s[t, low:high] = v2.reshape(count, ROWS, THIRD)

    def blend():
        scores = sc[...] * SCALE
        block = lax.broadcasted_iota(jnp.int32, scores.shape, 0) + 2 * chip - REACH
        usable = (block >= 0) & (block < nq) & (block >= q - REACH) & (block <= q + REACH)
        scores = jnp.where(usable, scores, -1e30)
        e = jnp.exp(scores - jnp.max(scores, 0, keepdims=True))
        p = (e * (1.0 / jnp.sum(e, 0, keepdims=True))).astype(BF16).reshape(SLOTS * ROWS, 128)
        for t in range(3):
            spread = dot(p, hmt[t]).reshape(SLOTS, ROWS, THIRD)
            a2s[t] = jnp.sum(spread * v2s[t].astype(F32), 0).astype(BF16)

    def final(step):
        o2 = dot(a2s[0], wf[12].reshape(THIRD, D))
        for t in range(1, 3):
            o2 = o2 + dot(a2s[t], wf[12 + t].reshape(THIRD, D))
        h2 = h1s[...] + mvec[5] * o2
        v = dot_t(fin[...], layer_norm(h2).astype(BF16))
        velocity[step] = v
        below = jnp.where(q > 0, levels[jnp.maximum(q - 1, 0)], 0)
        u = zcur[...] + ((below - levels[q]).astype(F32) / LEVELS) * v
        us[step] = u
        head = q > 0
        tail = q == nq - 1
        if step < STEPS - 1:
            ub[0] = u.astype(BF16)
            ub[1] = fresh[step].astype(BF16)
            for dx in range(NX):
                for dz in range(2):
                    back = SLOT[-dx % NX, dz]
                    here = SLOT[dx, dz]
                    send(ub.at[0], tok.at[step + 1, back], u_s.at[0, here], u_r.at[back],
                         q - 1, peer(dx, dz), head)
                    if here:
                        send(ub.at[1], tok.at[step + 1, back], u_s.at[1, here], u_r.at[back],
                             q, peer(dx, dz), tail)
        send(us.at[step], zf.at[step], v_s.at[step], v_r.at[step], q - 1, s, head)

    def arrive(step):
        arrived(zf.at[step], v_r.at[step], q < nq - 1)

        @pl.when(q == nq - 1)
        def _():
            zf[step] = fresh[step]

    cross_out(1)
    embed(0,0,1,2,3)
    onward(0,0)
    onward(1,0)
    embed(0,4,5,6,7)
    cross_in(0)
    cross_out(2)
    project(0)
    pass_on(0,0)
    far_in(0,0)
    project(1,2)
    pass_on(1,0)
    far_in(1,0)
    attend(0,2)
    onward(2,0)
    cross_in(1)
    cross_out(3)
    attend(0,3)
    onward(0,1)
    pass_on(0,1,2)
    attend(0,1)
    pass_on(1,1)
    far_in(2,0)
    pass_on(2,0)
    attend(0,0)
    far_in(0,1)
    pass_on(1,2)
    onward(3,0)
    cross_in(2)
    onward(1,1)
    pass_on(0,3)
    far_in(1,1)
    pass_on(0,4)
    pass_on(2,1,2)
    cross_in(3)
    pass_on(3,0)
    far_in(3,0)
    onward(2,1)
    pass_on(1,3)
    complete(0)
    middle(0)
    pass_on(3,1)
    pass_on(1,4)
    far_in(2,1)
    onward(3,1)
    pass_on(3,2)
    pass_on(2,3)
    complete(1)
    queries(0)
    relay(0,1,2)
    far_in(3,1)
    pass_on(2,4)
    complete(2)
    relay(0,0,3)
    relayed(0,1,2,0,3)
    keys(0,(0,10))
    pass_on(3,3)
    values(0,(0,10))
    pass_on(3,4)
    blend()
    complete(3)
    final(0)
    embed(1, 0, 1, 2, 3, 4, 5, 6, 7)
    project(0, 1, 2)
    attend(1, 2)
    attend(1, 3)
    attend(1, 1)
    attend(1, 0)
    arrive(0)
    zcur[...] = zf[0]
    middle(1)
    queries(1)
    keys(1, (4, 6))
    values(1, (4, 6))
    relay(1, 1, 2)
    relayed(1, 1, 2)
    keys(1, (2, 4), (6, 8))
    relay(1, 0, 3)
    values(1, (2, 4), (6, 8))
    relayed(1, 0, 3)
    keys(1, (0, 2), (8, 10))
    values(1, (0, 2), (8, 10))
    blend()
    final(1)
    arrive(1)
    after[...] = zf[1]

    for copy, when in sends:
        if when is None:
            copy.wait_send()
        else:
            pl.when(when)(copy.wait_send)


def solution(mesh):
    nq = mesh.shape["queue"]

    def local(latents, fresh_noise, levels, modulation_weight, embed_weight, attention_weights, final_weight):
        dma = pltpu.SemaphoreType.DMA
        vmem = pl.BlockSpec(memory_space=pltpu.VMEM)
        after, velocity = pl.pallas_call(
            functools.partial(kernel, nq),
            out_shape=(
                jax.ShapeDtypeStruct((16, ROWS), F32),
                jax.ShapeDtypeStruct((STEPS, 16, ROWS), F32),
            ),
            in_specs=[pl.BlockSpec(memory_space=pltpu.SMEM)] + [vmem] * 5 + [pl.BlockSpec(memory_space=pl.ANY)],
            out_specs=(vmem, vmem),
            scratch_shapes=[
                pltpu.VMEM((16, SPACE, ROWS, D), BF16),
                pltpu.VMEM((3, 3, ROWS, D), BF16),
                pltpu.VMEM((STEPS, SPACE, 16, ROWS), BF16),
                pltpu.VMEM((STEPS, 16, ROWS), F32),
                pltpu.VMEM((16, ROWS), F32),
                pltpu.VMEM((SPACE, 1, 2 * D), F32),
                pltpu.VMEM((8, 2 * D), F32),
                pltpu.VMEM((1, 2 * D), F32),
                pltpu.VMEM((6, 1, D), F32),
                pltpu.VMEM((SPACE, ROWS, D), BF16),
                pltpu.VMEM((SPACE * ROWS, 144), BF16),
                pltpu.VMEM((SPACE * ROWS, 144), BF16),
                pltpu.VMEM((SPACE * ROWS, 144), BF16),
                pltpu.VMEM((STEPS, SPACE, ROWS, 144), BF16),
                pltpu.VMEM((STEPS, SPACE, ROWS, 144), BF16),
                pltpu.VMEM((ROWS, D), F32),
                pltpu.VMEM((STEPS, 10, ROWS, D), BF16),
                pltpu.VMEM((3, ROWS, THIRD), BF16),
                pltpu.VMEM((3, ROWS, THIRD), BF16),
                pltpu.VMEM((SLOTS, ROWS, 128), F32),
                pltpu.VMEM((3, SLOTS, ROWS, THIRD), BF16),
                pltpu.VMEM((3, THIRD, 128), BF16),
                pltpu.VMEM((3, 128, THIRD), BF16),
                pltpu.VMEM((2, 16, ROWS), BF16),
                pltpu.VMEM((STEPS, 16, ROWS), F32),
                dma((6,)),
                dma((7,)), dma((SPACE,)),
                dma((7,)), dma((SPACE,)),
                dma((ROUNDS,)), dma((ROUNDS,)),
                dma((ROUNDS, 2, 2)), dma((ROUNDS, 2, 2)),
                dma((ROUNDS, 2)), dma((ROUNDS, 2)),
                dma((ROUNDS, 5)), dma((ROUNDS, 5)),
                dma((ROUNDS, 10)), dma((ROUNDS, 10)),
                dma((STEPS, 7)), dma((STEPS, SPACE)),
                dma((STEPS, 4)), dma((STEPS, 4)),
                dma((STEPS, 5)), dma((STEPS, 5)),
                dma((2, SPACE)), dma((SPACE,)),
                dma((STEPS,)), dma((STEPS,)),
            ],
            compiler_params=pltpu.CompilerParams(
                collective_id=0, has_side_effects=True, vmem_limit_bytes=56 << 20
            ),
            name="denoise",
        )(
            levels, latents[0].T, jnp.swapaxes(fresh_noise, 1, 2), modulation_weight.T, embed_weight,
            final_weight.T, attention_weights.reshape(8, 3, ROWS, D),
        )
        return after.T[None], jnp.swapaxes(velocity, 1, 2)[:, None]

    in_specs = (
        P("queue", "space", None),
        P(None, "space", None),
        P(),
        P(None, "space"),
        P(),
        P(None, "space", None),
        P(),
    )
    out_specs = (P("queue", "space", None), P(None, "queue", "space", None))
    return jax.shard_map(local, mesh=mesh, in_specs=in_specs, out_specs=out_specs, check_vma=False)
```

time: 143 us -> 113 us (0.79)
  the two profiles are of different devices: /device:TPU:201 before, /device:TPU:57 now
where the time goes in v2:
time: 113 us
  Pallas kernels  110 us (97%)
  local copies, waits for them, and re-layouts  2.62 us (2%)
    pallas_call x1, Pallas kernels, local(): pl.pallas_call(functools.partial(kernel, nq), out_shape=(jax.ShapeDtypeSt...  110 us
    unnamed x2, local copies, waits for them, and re-layouts  2.62 us

profile of v2, /device:TPU:57, one launch (start us, length us, event | category | flops | bytes accessed | tf_op | source)
XLA Modules:
  0.0 112.8 jit_solution(17551325241745886693)
XLA Ops:
  0.6 109.6 %denoise.1 = (f32[16,48]{1,0:T(8,128)}, f32[2,16,48]{2,1,0:T(8,128)}) custom-call(s32[64]{0:T(128)} %levels.1, f32[16,48]{1,0:T(8,128)} %bitcast.20, f32[2,16,48]{2,1,0:T(8,128)} %bitcast.18, bf16[864,256]{1,0:T(8,128)(2,1)} %bitcast.16, bf16[16,1152]{1,0:T(8,128)(2,1)} %emb.1, bf16[16,1152]{1,0:T(8,128)(2,1)} %bitcast.17, bf16[8,3,48,1152]{3,2,1,0:T(8,128)(2,1)} %bitcast.15), custom_call_target="tpu_custom_call" | custom-call | tf_op jit(solution)/shard_map/denoise/pallas_call | solution.py:513
  110.2 1.3 %copy.12 = f32[1,48,16]{1,2,0:T(8,128)} copy(f32[1,48,16]{1,2,0:T(8,128)} %bitcast.21) | data formatting | bytes 6144
  111.5 1.3 %copy.13 = f32[2,1,48,16]{2,3,1,0:T(8,128)} copy(f32[2,1,48,16]{2,3,1,0:T(8,128)} %bitcast.19) | data formatting | bytes 12288

commit v3 on v2

--- a/solution.py
+++ b/solution.py
@@ -65,7 +65,7 @@
     after, velocity,
     wf, ws, tok, zf, zcur, mods, mstage, mline, mvec, n1s, qs, ks, vs, a1s, a1r,
     h1s, n2b, q2s, a2s, sc, v2s, hm, hmt, ub, us,
-    lsem, lat_s, lat_r, mod_s, mod_r, z_s, z_r, x_s, x_r, f_s, f_r, y_s, y_r, c_s, c_r,
+    lsem, lat_s, lat_r, mod_s, mod_r, w_s, z_r, x_r, f_r, y_r, c_r,
     a_s, a_r, n_s, n_r, b_s, b_r, u_s, u_r, v_s, v_r,
 ):
     q = lax.axis_index("queue")
@@ -95,13 +95,17 @@
             device_id=(to_q, to_s), device_id_type=MESH,
         )
 
-    def send(src, dst, ss, rs, to_q, to_s, when=None):
+    def send(src, dst, ss, rs, to_q, to_s, when=None, grouped=False):
         copy = remote(src, dst, ss, rs, to_q, to_s)
         if when is None:
             copy.start()
         else:
             pl.when(when)(copy.start)
-        sends.append((copy, when))
+        if not grouped:
+            sends.append((copy, when))
+
+    def left(src, ss, when=None):
+        sends.append((remote(src, src, ss, ss, q, s), when))
 
     def arrived(dst, rs, when=None):
         copy = remote(dst, dst, rs, rs, q, s)
@@ -131,7 +135,7 @@
     signal(sibling, s)
     signal(mirror, peer(0, 1))
     expected = len(PEERS) + 4
-    for dc in CHIPS:
+    for dc in (-1, 1):
         there = (chip + dc >= 0) & (chip + dc < chips)
 
         @pl.when(there)
@@ -176,10 +180,12 @@
 
     for i, (dx, dz) in enumerate(PEERS):
         back = SLOT[-dx % NX, dz]
-        send(tok.at[0, 0], tok.at[0, back], lat_s.at[i], lat_r.at[back], q, peer(dx, dz))
+        send(tok.at[0, 0], tok.at[0, back], lat_s.at[0], lat_r.at[0], q, peer(dx, dz), grouped=True)
+    left(tok.at[0, 0:7], lat_s.at[0])
     for i, (dx, dz) in enumerate(PEERS):
         back = SLOT[-dx % NX, dz]
-        send(mline, mods.at[s], mod_s.at[i], mod_r.at[back], q, peer(dx, dz))
+        send(mline, mods.at[s], mod_s.at[0], mod_r.at[0], q, peer(dx, dz), grouped=True)
+    left(mods.at[0:7], mod_s.at[0])
     mods[s] = mline[...]
 
     def chunk(i, p, c):
@@ -187,19 +193,19 @@
 
     def own_out(i):
         j = chunk(i, parity, core)
-        send(wf.at[j, 0], wf.at[j, 1], x_s.at[i, 0, 0], x_r.at[i, 0, 0], q, peer(1, 0))
-        send(wf.at[j, 0], wf.at[j, 2], x_s.at[i, 0, 1], x_r.at[i, 0, 1], q, peer(3, 0))
+        send(wf.at[j, 0], wf.at[j, 1], w_s.at[0], x_r.at[i, 0, 0], q, peer(1, 0), grouped=True)
+        send(wf.at[j, 0], wf.at[j, 2], w_s.at[0], x_r.at[i, 0, 1], q, peer(3, 0), grouped=True)
 
     def cross_out(i):
         j = chunk(i, 1 - parity, core)
-        send(wf.at[j, 0], wf.at[j, 4], z_s.at[i], z_r.at[i], mirror, peer(0, 1))
+        send(wf.at[j, 0], wf.at[j, 4], w_s.at[0], z_r.at[i], mirror, peer(0, 1), grouped=True)
 
     def share(i, part):
         j = chunk(i, parity, core)
         at = pl.ds(*PARTS[part])
         to = beside if part in OVER_Z else ahead
-        send(wf.at[j, at], wf.at[j, at], y_s.at[i, part], y_r.at[i, part], to, s)
-        send(wf.at[j, at], wf.at[j, at], c_s.at[i, part], c_r.at[i, part], sibling, s)
+        send(wf.at[j, at], wf.at[j, at], w_s.at[0], y_r.at[i, part], to, s, grouped=True)
+        send(wf.at[j, at], wf.at[j, at], w_s.at[1], c_r.at[i, 0], sibling, s, grouped=True)
 
     def onward(i, half):
         j = chunk(i, parity, core)
@@ -207,7 +213,7 @@
         arrived(wf.at[j, base + 1], x_r.at[i, half, 0])
         arrived(wf.at[j, base + 2], x_r.at[i, half, 1])
         to = lax.rem(x + 1 + 2 * core, NX) * 2 + zh
-        send(wf.at[j, base + 1 + core], wf.at[j, base + 3], f_s.at[i, half], f_r.at[i, half], q, to)
+        send(wf.at[j, base + 1 + core], wf.at[j, base + 3], w_s.at[0], f_r.at[i, half], q, to, grouped=True)
         share(i, 3 * half)
 
     def far_in(i, half):
@@ -218,8 +224,8 @@
     def cross_in(i):
         j = chunk(i, parity, core)
         arrived(wf.at[j, 4], z_r.at[i])
-        send(wf.at[j, 4], wf.at[j, 5], x_s.at[i, 1, 0], x_r.at[i, 1, 0], q, peer(1, 0))
-        send(wf.at[j, 4], wf.at[j, 6], x_s.at[i, 1, 1], x_r.at[i, 1, 1], q, peer(3, 0))
+        send(wf.at[j, 4], wf.at[j, 5], w_s.at[0], x_r.at[i, 1, 0], q, peer(1, 0), grouped=True)
+        send(wf.at[j, 4], wf.at[j, 6], w_s.at[0], x_r.at[i, 1, 1], q, peer(3, 0), grouped=True)
         share(i, 2)
 
     def pass_on(i, *parts):
@@ -227,43 +233,46 @@
         for part in parts:
             at = pl.ds(*PARTS[part])
             arrived(wf.at[j, at], y_r.at[i, part])
-            send(wf.at[j, at], wf.at[j, at], c_s.at[i, 5 + part], c_r.at[i, 5 + part], sibling, s)
+            send(wf.at[j, at], wf.at[j, at], w_s.at[1], c_r.at[i, 1], sibling, s, grouped=True)
 
     def complete(i):
-        for half, p in ((0, parity), (5, 1 - parity)):
-            j = chunk(i, p, 1 - core)
-            for part in range(5):
-                arrived(wf.at[j, pl.ds(*PARTS[part])], c_r.at[i, half + part])
+        for half, p in ((0, parity), (1, 1 - parity)):
+            arrived(wf.at[chunk(i, p, 1 - core), 1:8], c_r.at[i, half])
+
+    for group in range(2):
+        left(wf.at[0:7], w_s.at[group])
 
     for load in loads[1:]:
         load.wait()
-    own_out(0)
+    for i in range(ROUNDS):
+        own_out(i)
     cross_out(0)
-    own_out(1)
-    own_out(2)
-    own_out(3)
-
-    for dx, dz in PEERS:
-        arrived(mods.at[peer(dx, dz)], mod_r.at[SLOT[dx, dz]])
+
+    arrived(mods.at[0:7], mod_r.at[0])
     for base in (0, 4):
         piece = base // 4 * 3
-        left = [mods[base + g][:, 0:D] for g in range(4)]
-        right = [mods[base + g][:, D : 2 * D] for g in range(4)]
-        mvec[piece] = left[0] + left[1]
-        mvec[piece + 1] = right[1] + left[2]
-        mvec[piece + 2] = right[2] + left[3]
+        lower = [mods[base + g][:, 0:D] for g in range(4)]
+        upper = [mods[base + g][:, D : 2 * D] for g in range(4)]
+        mvec[piece] = lower[0] + lower[1]
+        mvec[piece + 1] = upper[1] + lower[2]
+        mvec[piece + 2] = upper[2] + lower[3]
 
     loads[0].wait()
     lane = lax.broadcasted_iota(jnp.int32, (1, 144), 1)
     in_first = lane < HEAD
+    pick = (
+        lax.broadcasted_iota(jnp.int32, (16, 144), 1)
+        == lax.broadcasted_iota(jnp.int32, (16, 144), 0) + 128
+    ).astype(F32).astype(BF16)
 
     def embed(step, *slots):
         for r in slots:
-            if step == 0 and r:
-                arrived(tok.at[0, r], lat_r.at[r])
-            elif r:
-                arrived(tok.at[step, r], u_r.at[r])
-            elif step:
+            if step == 0:
+                if r == 1:
+                    arrived(tok.at[0, 1:8], lat_r.at[0])
+            elif r in (1, 4):
+                arrived(tok.at[step, r : 4 if r == 1 else SPACE], u_r.at[r // 4 + 1])
+            elif r == 0:
                 arrived(tok.at[step, 0], u_r.at[0], q < nq - 1)
 
                 @pl.when(q == nq - 1)
@@ -289,28 +298,37 @@
             p = (e * (1.0 / jnp.sum(e, -1, keepdims=True))).astype(BF16)
             heads.append(dot(p, vs[...]))
         a1 = jnp.where(in_first, heads[0], heads[1]).astype(BF16)
-        a1s[step, 2 * b : 2 * b + 2] = a1.reshape(2, ROWS, 144)
+        a1s[step, 2 * b : 2 * b + 2, 0:3] = a1[:, 0:128].reshape(2, 3, 16, 128)
+        for half in range(2):
+            rest = dot_t(pick, a1[half * ROWS : half * ROWS + ROWS])
+            a1s[step, 2 * b + half, 3, :, 0:ROWS] = rest.astype(BF16)
         for i, (dx, dz) in enumerate(PEERS):
             if SLOT[dx, dz] // 2 == b:
                 back = SLOT[-dx % NX, dz]
                 send(a1s.at[step, SLOT[dx, dz]], a1r.at[step, back],
-                     a_s.at[step, i], a_r.at[step, back], q, peer(dx, dz))
+                     a_s.at[step], a_r.at[step, back // 4], q, peer(dx, dz), grouped=True)
         if b == 0:
             a1r[step, 0] = a1s[step, 0]
+            left(a1s.at[step, 0:7], a_s.at[step])
 
     def middle(step):
         h0 = t_dot(tok[step, 0], emb[...])
-        o1 = dot(a1r[step, 0], wf[0:3, 0].reshape(144, D))
-        for r in range(1, SPACE):
-            arrived(a1r.at[step, r], a_r.at[step, r])
-            o1 = o1 + dot(a1r[step, r], wf[0:3, r].reshape(144, D))
+        o1 = jnp.zeros((ROWS, D), F32)
+        for r in range(SPACE):
+            if r in (1, 4):
+                arrived(a1r.at[step, r : 4 if r == 1 else SPACE], a_r.at[step, r // 4])
+            top = wf[0:3, r].reshape(144, D)[0:128]
+            o1 = o1 + dot(a1r[step, r, 0:3].reshape(ROWS, 128), top)
+        rest = jnp.concatenate([a1r[step, r, 3, :, 0:ROWS] for r in range(SPACE)], 0)
+        bottom = wf[2, :, 32:ROWS].reshape(128, D)
+        o1 = o1 + t_dot(rest, bottom)
         h1 = h0 + mvec[2] * o1
         h1s[...] = h1
         n2 = layer_norm(h1) * (1.0 + mvec[4]) + mvec[3]
         n2b[step, 4 + core] = n2.astype(BF16)
         own = n2b.at[step, 4 + core]
         send(own, own, b_s.at[step, 4], b_r.at[step, 4], sibling, s)
-        for i in (1, 2, 0, 3):
+        for i in (1, 2):
             dc = CHIPS[i]
             there = (chip + dc >= 0) & (chip + dc < chips)
             send(own, n2b.at[step, (2 - dc) * 2 + core], n_s.at[step, i], n_r.at[step, 3 - i],
@@ -322,6 +340,10 @@
             there = (chip + dc >= 0) & (chip + dc < chips)
             slot = (dc + 2) * 2 + core
             arrived(n2b.at[step, slot], n_r.at[step, i], there)
+            if i in (1, 2):
+                send(n2b.at[step, slot], n2b.at[step, (2 + 2 * dc) * 2 + core], n_s.at[step, 3 * (i - 1)],
+                     n_r.at[step, 3 * (i - 1)], (chip - dc) * 2 + core, s,
+                     there & (chip - dc >= 0) & (chip - dc < chips))
             wanted = there
             if dc == -2:
                 wanted = there & (core == 1)
@@ -347,24 +369,32 @@
             q2s[t] = dot_t(n2b[step, 4 + core], wf[3 + t].reshape(THIRD, D)).astype(BF16)
         arrived(n2b.at[step, 5 - core], b_r.at[step, 4])
 
+    def rows_of(step, groups):
+        blocks = [n2b[step, low:high] for low, high in groups]
+        blocks = blocks[0] if len(blocks) == 1 else jnp.concatenate(blocks, 0)
+        return blocks.shape[0], blocks.reshape(-1, D)
+
     def keys(step, *groups):
+        count, rows = rows_of(step, groups)
+        total = jnp.zeros((count * ROWS, 128), F32)
+        for t in range(3):
+            k2 = dot_t(rows, wf[6 + t].reshape(THIRD, D)).astype(BF16)
+            product = k2.reshape(count, ROWS, THIRD).astype(F32) * q2s[t].astype(F32)[None]
+            total = total + dot(product.astype(BF16).reshape(count * ROWS, THIRD), hm[t])
+        total = total.reshape(count, ROWS, 128)
+        at = 0
         for low, high in groups:
-            count = high - low
-            rows = n2b[step, low:high].reshape(count * ROWS, D)
-            total = jnp.zeros((count * ROWS, 128), F32)
-            for t in range(3):
-                k2 = dot_t(rows, wf[6 + t].reshape(THIRD, D)).astype(BF16)
-                product = k2.reshape(count, ROWS, THIRD).astype(F32) * q2s[t].astype(F32)[None]
-                total = total + dot(product.astype(BF16).reshape(count * ROWS, THIRD), hm[t])
-            sc[low:high] = total.reshape(count, ROWS, 128)
+            sc[low:high] = total[at : at + high - low]
+            at += high - low
 
     def values(step, *groups):
-        for low, high in groups:
-            count = high - low
-            rows = n2b[step, low:high].reshape(count * ROWS, D)
-            for t in range(3):
-                v2 = dot_t(rows, wf[9 + t].reshape(THIRD, D)).astype(BF16)
-                v2s[t, low:high] = v2.reshape(count, ROWS, THIRD)
+        count, rows = rows_of(step, groups)
+        for t in range(3):
+            v2 = dot_t(rows, wf[9 + t].reshape(THIRD, D)).astype(BF16).reshape(count, ROWS, THIRD)
+            at = 0
+            for low, high in groups:
+                v2s[t, low:high] = v2[at : at + high - low]
+                at += high - low
 
     def blend():
         scores = sc[...] * SCALE
@@ -396,11 +426,13 @@
                 for dz in range(2):
                     back = SLOT[-dx % NX, dz]
                     here = SLOT[dx, dz]
-                    send(ub.at[0], tok.at[step + 1, back], u_s.at[0, here], u_r.at[back],
-                         q - 1, peer(dx, dz), head)
+                    send(ub.at[0], tok.at[step + 1, back], u_s.at[0], u_r.at[(back > 0) + back // 4],
+                         q - 1, peer(dx, dz), head, grouped=True)
                     if here:
-                        send(ub.at[1], tok.at[step + 1, back], u_s.at[1, here], u_r.at[back],
-                             q, peer(dx, dz), tail)
+                        send(ub.at[1], tok.at[step + 1, back], u_s.at[1], u_r.at[(back > 0) + back // 4],
+                             q, peer(dx, dz), tail, grouped=True)
+            left(tok.at[0, 0:8], u_s.at[0], head)
+            left(tok.at[0, 0:7], u_s.at[1], tail)
         send(us.at[step], zf.at[step], v_s.at[step], v_r.at[step], q - 1, s, head)
 
     def arrive(step):
@@ -410,65 +442,67 @@
         def _():
             zf[step] = fresh[step]
 
+    embed(0, 0, 1, 2, 3)
+    onward(0, 0)
     cross_out(1)
-    embed(0,0,1,2,3)
-    onward(0,0)
-    onward(1,0)
-    embed(0,4,5,6,7)
+    embed(0, 4, 5, 6, 7)
+    onward(1, 0)
+    project(0)
     cross_in(0)
     cross_out(2)
-    project(0)
-    pass_on(0,0)
-    far_in(0,0)
-    project(1,2)
-    pass_on(1,0)
-    far_in(1,0)
-    attend(0,2)
-    onward(2,0)
+    pass_on(0, 0)
+    project(1, 2)
+    onward(2, 0)
+    attend(0, 2)
+    pass_on(1, 0)
+    onward(3, 0)
+    attend(0, 3)
+    pass_on(0, 2)
+    far_in(0, 0)
     cross_in(1)
     cross_out(3)
-    attend(0,3)
-    onward(0,1)
-    pass_on(0,1,2)
-    attend(0,1)
-    pass_on(1,1)
-    far_in(2,0)
-    pass_on(2,0)
-    attend(0,0)
-    far_in(0,1)
-    pass_on(1,2)
-    onward(3,0)
+    attend(0, 1)
+    pass_on(2, 0)
+    far_in(1, 0)
+    pass_on(3, 0)
+    attend(0, 0)
+    onward(0, 1)
+    pass_on(0, 1)
+    pass_on(1, 2)
+    far_in(2, 0)
     cross_in(2)
-    onward(1,1)
-    pass_on(0,3)
-    far_in(1,1)
-    pass_on(0,4)
-    pass_on(2,1,2)
+    pass_on(1, 1)
+    far_in(3, 0)
+    pass_on(0, 3)
+    onward(1, 1)
+    pass_on(2, 1)
+    pass_on(2, 2)
+    far_in(0, 1)
     cross_in(3)
-    pass_on(3,0)
-    far_in(3,0)
-    onward(2,1)
-    pass_on(1,3)
+    pass_on(3, 1)
+    onward(2, 1)
+    pass_on(1, 3)
+    far_in(1, 1)
+    pass_on(0, 4)
     complete(0)
     middle(0)
-    pass_on(3,1)
-    pass_on(1,4)
-    far_in(2,1)
-    onward(3,1)
-    pass_on(3,2)
-    pass_on(2,3)
+    onward(3, 1)
+    pass_on(2, 3)
+    pass_on(3, 2)
+    far_in(2, 1)
+    far_in(3, 1)
+    pass_on(1, 4)
     complete(1)
     queries(0)
-    relay(0,1,2)
-    far_in(3,1)
-    pass_on(2,4)
+    relay(0, 1, 2)
+    pass_on(3, 3)
+    pass_on(2, 4)
+    relay(0, 0, 3)
+    pass_on(3, 4)
     complete(2)
-    relay(0,0,3)
-    relayed(0,1,2,0,3)
-    keys(0,(0,10))
-    pass_on(3,3)
-    values(0,(0,10))
-    pass_on(3,4)
+    relayed(0, 1, 2, 0, 3)
+    keys(0, (0, 10))
+    values(0, (0, 10))
     blend()
     complete(3)
     final(0)
@@ -487,8 +521,8 @@
     relay(1, 1, 2)
     relayed(1, 1, 2)
     keys(1, (2, 4), (6, 8))
+    values(1, (2, 4), (6, 8))
     relay(1, 0, 3)
-    values(1, (2, 4), (6, 8))
     relayed(1, 0, 3)
     keys(1, (0, 2), (8, 10))
     values(1, (0, 2), (8, 10))
@@ -502,6 +536,11 @@
             copy.wait_send()
         else:
             pl.when(when)(copy.wait_send)
+
+
+def hand_out(after_in, velocity_in, after, velocity):
+    after[...] = after_in[...]
+    velocity[...] = velocity_in[...]
 
 
 def solution(mesh):
@@ -532,8 +571,8 @@
                 pltpu.VMEM((SPACE * ROWS, 144), BF16),
                 pltpu.VMEM((SPACE * ROWS, 144), BF16),
                 pltpu.VMEM((SPACE * ROWS, 144), BF16),
-                pltpu.VMEM((STEPS, SPACE, ROWS, 144), BF16),
-                pltpu.VMEM((STEPS, SPACE, ROWS, 144), BF16),
+                pltpu.VMEM((STEPS, SPACE, 4, 16, 128), BF16),
+                pltpu.VMEM((STEPS, SPACE, 4, 16, 128), BF16),
                 pltpu.VMEM((ROWS, D), F32),
                 pltpu.VMEM((STEPS, 10, ROWS, D), BF16),
                 pltpu.VMEM((3, ROWS, THIRD), BF16),
@@ -545,17 +584,14 @@
                 pltpu.VMEM((2, 16, ROWS), BF16),
                 pltpu.VMEM((STEPS, 16, ROWS), F32),
                 dma((6,)),
-                dma((7,)), dma((SPACE,)),
-                dma((7,)), dma((SPACE,)),
-                dma((ROUNDS,)), dma((ROUNDS,)),
-                dma((ROUNDS, 2, 2)), dma((ROUNDS, 2, 2)),
-                dma((ROUNDS, 2)), dma((ROUNDS, 2)),
-                dma((ROUNDS, 5)), dma((ROUNDS, 5)),
-                dma((ROUNDS, 10)), dma((ROUNDS, 10)),
-                dma((STEPS, 7)), dma((STEPS, SPACE)),
+                dma((1,)), dma((1,)),
+                dma((1,)), dma((1,)),
+                dma((2,)), dma((ROUNDS,)), dma((ROUNDS, 2, 2)), dma((ROUNDS, 2)),
+                dma((ROUNDS, 5)), dma((ROUNDS, 2)),
+                dma((STEPS,)), dma((STEPS, 2)),
                 dma((STEPS, 4)), dma((STEPS, 4)),
                 dma((STEPS, 5)), dma((STEPS, 5)),
-                dma((2, SPACE)), dma((SPACE,)),
+                dma((2,)), dma((3,)),
                 dma((STEPS,)), dma((STEPS,)),
             ],
             compiler_params=pltpu.CompilerParams(
@@ -566,6 +602,9 @@
             levels, latents[0].T, jnp.swapaxes(fresh_noise, 1, 2), modulation_weight.T, embed_weight,
             final_weight.T, attention_weights.reshape(8, 3, ROWS, D),
         )
+        after, velocity = pl.pallas_call(
+            hand_out, out_shape=(after, velocity), in_specs=[vmem] * 2, out_specs=(vmem, vmem), name="hand_out"
+        )(after, velocity)
         return after.T[None], jnp.swapaxes(velocity, 1, 2)[:, None]
 
     in_specs = (

time: 113 us -> 104 us (0.920)
  Pallas kernels: 110 us -> 103 us
  local copies, waits for them, and re-layouts: 2.62 us -> 0 us
    pallas_call x1, Pallas kernels: 110 us -> 101 us  [local(): pl.pallas_call(functools.partial(kernel, nq), out_shape=(jax.ShapeDtypeSt...]
    unnamed x2 -> x0, local copies, waits for them, and re-layouts: 2.62 us -> none
    pallas_call x0 -> x1, Pallas kernels: none -> 1.35 us  [local(): pl.pallas_call(hand_out, out_shape=(after, velocity), in_specs=[vmem] * 2...]
where the time goes in v3:
time: 104 us; the launch traced here: 103 us
  Pallas kernels  103 us (99%)
    pallas_call x1, Pallas kernels, local(): pl.pallas_call(functools.partial(kernel, nq), out_shape=(jax.ShapeDtypeSt...  101 us

profile of v3, /device:TPU:57, one launch (start us, length us, event | category | flops | bytes accessed | tf_op | source)
XLA Modules:
  0.0 103.3 jit_solution(5865778471811883066)
XLA Ops:
  0.6 101.3 %denoise.1 = (f32[16,48]{1,0:T(8,128)}, f32[2,16,48]{2,1,0:T(8,128)}) custom-call(s32[64]{0:T(128)} %levels.1, f32[16,48]{1,0:T(8,128)} %bitcast.19, f32[2,16,48]{2,1,0:T(8,128)} %bitcast.18, bf16[864,256]{1,0:T(8,128)(2,1)} %bitcast.16, bf16[16,1152]{1,0:T(8,128)(2,1)} %emb.1, bf16[16,1152]{1,0:T(8,128)(2,1)} %bitcast.17, bf16[8,3,48,1152]{3,2,1,0:T(8,128)(2,1)} %bitcast.15), custom_call_target="tpu_custom_call" | custom-call | tf_op jit(solution)/shard_map/denoise/pallas_call | solution.py:552
  102.0 1.3 %hand_out.1 = (f32[16,48]{1,0:T(8,128)}, f32[2,16,48]{2,1,0:T(8,128)}) custom-call(f32[16,48]{1,0:T(8,128)} %get-tuple-element.6.after_in, f32[2,16,48]{2,1,0:T(8,128)} %get-tuple-element.7.velocity_in), custom_call_target="tpu_custom_call" | custom-call | tf_op jit(solution)/shard_map/hand_out/pallas_call | solution.py:605

commit v4 on v3

--- a/solution.py
+++ b/solution.py
@@ -279,8 +279,10 @@
                 def _():
                     tok[step, 0] = fresh[step - 1].astype(BF16)
 
-            h0 = t_dot(tok[step, r], emb[...])
-            n1s[r] = (layer_norm(h0) * (1.0 + mvec[1]) + mvec[0]).astype(BF16)
+        low, count = slots[0], len(slots)
+        h0 = jnp.concatenate([t_dot(tok[step, r], emb[...]) for r in slots], 0)
+        n1 = (layer_norm(h0) * (1.0 + mvec[1]) + mvec[0]).astype(BF16)
+        n1s[low : low + count] = n1.reshape(count, ROWS, D)
 
     def project(*indices):
         for index in indices:
@@ -289,7 +291,7 @@
             ).astype(BF16)
 
     def attend(step, b):
-        query = qs[b * 96 : b * 96 + 96, :]
+        query = qs[b * 192 : b * 192 + 192, :]
         heads = []
         for h in range(2):
             mine = in_first if h == 0 else ~in_first
@@ -298,12 +300,12 @@
             p = (e * (1.0 / jnp.sum(e, -1, keepdims=True))).astype(BF16)
             heads.append(dot(p, vs[...]))
         a1 = jnp.where(in_first, heads[0], heads[1]).astype(BF16)
-        a1s[step, 2 * b : 2 * b + 2, 0:3] = a1[:, 0:128].reshape(2, 3, 16, 128)
-        for half in range(2):
-            rest = dot_t(pick, a1[half * ROWS : half * ROWS + ROWS])
-            a1s[step, 2 * b + half, 3, :, 0:ROWS] = rest.astype(BF16)
+        a1s[step, 4 * b : 4 * b + 4, 0:3] = a1[:, 0:128].reshape(4, 3, 16, 128)
+        for part in range(4):
+            rest = dot_t(pick, a1[part * ROWS : part * ROWS + ROWS])
+            a1s[step, 4 * b + part, 3, :, 0:ROWS] = rest.astype(BF16)
         for i, (dx, dz) in enumerate(PEERS):
-            if SLOT[dx, dz] // 2 == b:
+            if SLOT[dx, dz] // 4 == b:
                 back = SLOT[-dx % NX, dz]
                 send(a1s.at[step, SLOT[dx, dz]], a1r.at[step, back],
                      a_s.at[step], a_r.at[step, back // 4], q, peer(dx, dz), grouped=True)
@@ -453,15 +455,13 @@
     pass_on(0, 0)
     project(1, 2)
     onward(2, 0)
-    attend(0, 2)
+    attend(0, 1)
     pass_on(1, 0)
     onward(3, 0)
-    attend(0, 3)
     pass_on(0, 2)
     far_in(0, 0)
     cross_in(1)
     cross_out(3)
-    attend(0, 1)
     pass_on(2, 0)
     far_in(1, 0)
     pass_on(3, 0)
@@ -506,10 +506,9 @@
     blend()
     complete(3)
     final(0)
-    embed(1, 0, 1, 2, 3, 4, 5, 6, 7)
+    embed(1, 0, 1, 2, 3)
+    embed(1, 4, 5, 6, 7)
     project(0, 1, 2)
-    attend(1, 2)
-    attend(1, 3)
     attend(1, 1)
     attend(1, 0)
     arrive(0)

time: 104 us -> 103 us (level)
  no operation moved by 1% of the time
where the time goes in v4:
time: 103 us
  Pallas kernels  102 us (99%)
    pallas_call x1, Pallas kernels, local(): pl.pallas_call(functools.partial(kernel, nq), out_shape=(jax.ShapeDtypeSt...  101 us

profile of v4, /device:TPU:57, one launch (start us, length us, event | category | flops | bytes accessed | tf_op | source)
XLA Modules:
  0.0 102.7 jit_solution(7679253044078046176)
XLA Ops:
  0.6 100.7 %denoise.1 = (f32[16,48]{1,0:T(8,128)}, f32[2,16,48]{2,1,0:T(8,128)}) custom-call(s32[64]{0:T(128)} %levels.1, f32[16,48]{1,0:T(8,128)} %bitcast.19, f32[2,16,48]{2,1,0:T(8,128)} %bitcast.18, bf16[864,256]{1,0:T(8,128)(2,1)} %bitcast.16, bf16[16,1152]{1,0:T(8,128)(2,1)} %emb.1, bf16[16,1152]{1,0:T(8,128)(2,1)} %bitcast.17, bf16[8,3,48,1152]{3,2,1,0:T(8,128)(2,1)} %bitcast.15), custom_call_target="tpu_custom_call" | custom-call | tf_op jit(solution)/shard_map/denoise/pallas_call | solution.py:551
  101.3 1.3 %hand_out.1 = (f32[16,48]{1,0:T(8,128)}, f32[2,16,48]{2,1,0:T(8,128)}) custom-call(f32[16,48]{1,0:T(8,128)} %get-tuple-element.6.after_in, f32[2,16,48]{2,1,0:T(8,128)} %get-tuple-element.7.velocity_in), custom_call_target="tpu_custom_call" | custom-call | tf_op jit(solution)/shard_map/hand_out/pallas_call | solution.py:604
